TPU v7x, 128 devices: a whole 4x4x4 slice. The times are simulated.
128 devices in a mesh: rep: 2 (over x_lo), row: 64 (over z, y, x_hi, core).
Axes of the slice: x: 4 (x_hi: 2, x_lo: 2; x = x_hi * 2 + x_lo), y: 4, z: 4, core: 2. Of those that a mesh axis runs over, the one named last changes fastest.
Arguments:
- features: bfloat16 [131072, 128], P(('row', 'rep')), may hold values from -6 to 6
- blocks: bfloat16 [64, 2, 64, 2, 256, 256], P('row', 'rep'), may hold values from 0 to 0.049804688
- codes: int32 [64, 2, 64, 2], P('row', 'rep'), may hold values from 0 to 31, as said below
- counts: int32 [64, 2, 64], P('row', 'rep'), may hold values from 0 to 2
- weight: bfloat16 [128, 256], replicated, may hold values from -0.5 to 0.5
- bias: float32 [256], replicated, may hold values from -3 to 3
Outputs:
- mixed: bfloat16 [131072, 256], P(('row', 'rep'))
Inputs may be any that keep to these rules, and one draw needn't show every extreme that they name: `codes`: each slot names row block and column block as rowblock * 4 + colblock; the slots of one device and section are distinct; slots at or past the section's count are unused.
All inputs are finite; a program needn't handle non-finite values.
Results may differ from a plain program's by a relative error of at most 0.014.
Values may be sent and summed in bfloat16 or wider, within the bound.
No kernel may reach another device: no remote copies, remote signals or barrier semaphores. Data moves between devices by JAX's collectives and lax.ppermute only.
A program may use at most 128 MiB of HBM per device.

v0:
```python
import functools

import jax
import jax.numpy as jnp
import numpy as np
from jax import lax
from jax.experimental import pallas as pl
from jax.experimental.pallas import tpu as pltpu
from jax.sharding import PartitionSpec as P

DIMS = (4, 4, 2, 2)
SLOTS = 2
VMEM_LIMIT = 4 * 2**20
WIDTH = (2, 4)

HOME = (0, 0, 0)
ROUNDS = (
    (("P1", (HOME,)), ("M1", (HOME,)), ("X", (HOME,)), ("P2", (HOME,)), ("M2", (HOME,))),
    (
        ("P1", ((0, 0, 3), (0, 0, 1))),
        ("M1", ((0, 1, 0), (0, 0, 1))),
        ("X", ((0, 0, 3), (0, 0, 1))),
        ("P2", ((1, 0, 0), (0, 1, 0))),
        ("M2", ((1, 0, 0), (0, 0, 1))),
    ),
    (
        ("P1", ((1, 0, 1), (0, 0, 2))),
        ("M1", ((0, 1, 3), (1, 1, 0))),
        ("X", ((0, 2, 0), (0, 1, 1))),
        ("P2", ((1, 3, 0), (1, 1, 0))),
        ("M2", ((0, 2, 0), (0, 1, 1))),
    ),
    (
        ("D1", ((1, 0, 2),)),
        ("P1", ((1, 0, 2),)),
        ("X", ((0, 2, 1),)),
        ("P2", ((0, 2, 3), (1, 2, 0))),
        ("M2", ((1, 2, 0),)),
    ),
)
MIRROR = True
LATE = ((), (), ('P1', 'P2'), ('M2',))
STEPS = {"P1": (0, 1), "M1": (0, -1), "D1": (0, 2), "P2": (1, 1), "M2": (1, -1)}


def row_of(place):
    return int(np.ravel_multi_index(place, DIMS))


def pairs_of(channel):
    pairs = []
    for place in np.ndindex(*DIMS):
        to = list(place)
        if channel == "X":
            to[2] = 1 - to[2]
        elif channel == "C":
            to[3] = 1 - to[3]
        else:
            axis, by = STEPS[channel]
            axis = (axis + place[2]) % 2
            to[axis] = (to[axis] + by * (1 - 2 * place[3] * MIRROR)) % DIMS[axis]
        pairs.append((row_of(place), row_of(to)))
    return pairs


def arrived(channel, unit):
    t, a, b = unit
    if channel == "X":
        return (1 - t, b, a)
    axis, by = STEPS[channel]
    return (t, (a - by) % 4, b) if axis == 0 else (t, a, (b - by) % 4)


def send(x, channel):
    return lax.ppermute(x, "row", pairs_of(channel))


def owner_of(where, unit, core_flip):
    t, a, b = unit
    row = where[0]
    h = (row >> 1) & 1
    sign = 1 - 2 * ((row & 1) ^ core_flip)
    if MIRROR:
        a, b = a * sign, b * sign
    z = ((row >> 4) + a + h * (b - a)) & 3
    y = (((row >> 2) & 3) + b + h * (a - b)) & 3
    return (((z * 4 + y) * 2 + (h ^ t)) << 1) + ((row & 1) ^ core_flip)


def pack_kernel(layout, begin, block, where, codes, *refs):
    arrays, out = refs[: len(layout)], refs[-1]
    n = begin
    for array, units in zip(arrays, layout):
        size = array.shape[0] // len(units)
        for at, unit in enumerate(units):
            owner = owner_of(where, unit, 0)
            for k in range(SLOTS):

                @pl.when(k < codes[SLOTS, owner])
                def _():
                    start = pl.multiple_of(at * size + (codes[k, owner] & 3) * block, block)
                    out[n * SLOTS + k] = array[pl.ds(start, block), :]

            n += 1


def pack(group, where, codes, block, total, into=None):
    arrays, layout = [x for x, _ in group], tuple(us for _, us in group)
    channels = arrays[0].shape[1]
    count = sum(map(len, layout))
    vmem = pl.BlockSpec(memory_space=pltpu.VMEM)
    operands = [where, codes, *arrays] + ([] if into is None else [into])
    return pl.pallas_call(
        functools.partial(pack_kernel, layout, 0 if into is None else total - count, block),
        out_shape=jax.ShapeDtypeStruct((total * SLOTS, block, channels), jnp.bfloat16),
        in_specs=[pl.BlockSpec(memory_space=pltpu.SMEM)] * 2 + [vmem] * (len(operands) - 2),
        out_specs=vmem,
        input_output_aliases={} if into is None else {len(operands) - 1: 0},
        cost_estimate=pl.CostEstimate(
            flops=0, bytes_accessed=count * SLOTS * block * channels * 4, transcendentals=0
        ),
        compiler_params=pltpu.CompilerParams(vmem_limit_bytes=VMEM_LIMIT),
        name="pack",
    )(*operands)


def terms_kernel(layout, half, where, codes, blocks, *refs):
    arrays, refs = refs[: len(layout)], refs[len(layout) :]
    total_in = None
    if len(refs) > 2:
        total_in, refs = refs[0], refs[1:]
    total, owners = refs
    block = blocks.shape[-1]
    base = where[1] * 4
    size = total.shape[0]

    for n, (unit, flip) in enumerate([(u, flip) for us, flip in layout for u in us]):
        owners[n] = owner_of(where, unit, flip)
    if total_in is None:
        total[...] = jnp.zeros_like(total)
    elif total_in.shape == total.shape:
        total[...] = total_in[...]
    else:
        total[...] = total_in[half * size : (half + 1) * size, :]

    def target_of(owner, k):
        return ((codes[k, owner] >> 2) + base) & 7

    def counts(owner, k):
        live = k < codes[SLOTS, owner]
        return live if half is None else live & (target_of(owner, k) >> 2 == half)

    def sweep(begin, count, features, width):
        def products(tasks):
            found = []
            for i, k in tasks:
                owner = owners[begin + i]
                target = target_of(owner, k)
                if half is not None:
                    target = target & 3
                rows = pl.ds(pl.multiple_of(target * block, block), block)
                product = jnp.dot(
                    blocks[owner, k], features(i, codes[k, owner], k), preferred_element_type=jnp.float32
                )
                found.append((rows, product))
            for rows, product in found:
                total[rows, :] += product

        def some(first, units):
            tasks = [(first + i, k) for i in range(units) for k in range(SLOTS)]
            whole = functools.reduce(jnp.logical_and, [counts(owners[begin + i], k) for i, k in tasks])

            @pl.when(whole)
            def _():
                products(tasks)

            @pl.when(jnp.logical_not(whole))
            def _():
                def one(task, carry):
                    i, k = first + task // SLOTS, task % SLOTS

                    @pl.when(counts(owners[begin + i], k))
                    def _():
                        products([(i, k)])

                    return carry

                lax.fori_loop(0, len(tasks), one, 0)

        width = min(count, width if half is None else 1)
        steps = count // width
        if steps == 1:
            some(0, width)
        elif steps:

            def step(n, carry):
                some(n * width, width)
                return carry

            lax.fori_loop(0, steps, step, 0)
        if count % width:
            some(steps * width, count % width)

    begin = 0
    for array, (us, flip) in zip(arrays, layout):
        unit_rows = array.shape[0] // len(us)

        def features(i, code, k, array=array, unit_rows=unit_rows, flip=flip):
            if flip:
                return array[i * SLOTS + k]
            return array[pl.ds(pl.multiple_of(i * unit_rows + (code & 3) * block, block), block), :]

        sweep(begin, len(us), features, WIDTH[flip])
        begin += len(us)


def terms(group, packed, running, where, codes, blocks, half=None):
    sources = [(x, us, 0) for x, us in group] + [(x, us, 1) for x, us in packed]
    layout = tuple((us, flip) for _, us, flip in sources)
    block = blocks.shape[-1]
    channels = sources[0][0].shape[-1]
    n = sum(len(us) for us, _ in layout) * SLOTS
    vmem = pl.BlockSpec(memory_space=pltpu.VMEM)
    operands = [where, codes, blocks] + [x for x, _, _ in sources] + ([] if running is None else [running])
    return pl.pallas_call(
        functools.partial(terms_kernel, layout, half),
        out_shape=jax.ShapeDtypeStruct((8 * block if half is None else 4 * block, channels), jnp.float32),
        in_specs=[pl.BlockSpec(memory_space=pltpu.SMEM)] * 2 + [vmem] * (len(operands) - 2),
        out_specs=vmem,
        scratch_shapes=[pltpu.SMEM((n // SLOTS,), jnp.int32)],
        compiler_params=pltpu.CompilerParams(vmem_limit_bytes=VMEM_LIMIT),
        cost_estimate=pl.CostEstimate(
            flops=2 * n * block * block * channels,
            bytes_accessed=n * (block * block + block * channels) * 2,
            transcendentals=0,
        ),
        name="terms",
    )(*operands)


def load_kernel(source, out, sem):
    copy = pltpu.make_async_copy(source, out, sem)
    copy.start()
    copy.wait()


def load(blocks):
    return pl.pallas_call(
        load_kernel,
        out_shape=pltpu.VMEM(blocks.shape, blocks.dtype),
        in_specs=[pl.BlockSpec(memory_space=pltpu.HBM)],
        out_specs=pl.BlockSpec(memory_space=pltpu.VMEM),
        scratch_shapes=[pltpu.SemaphoreType.DMA(())],
        compiler_params=pltpu.CompilerParams(vmem_limit_bytes=VMEM_LIMIT),
        cost_estimate=pl.CostEstimate(flops=0, bytes_accessed=2 * blocks.size, transcendentals=0),
        name="load",
    )(pltpu.with_memory_space_constraint(blocks, pltpu.HBM))


def after(xs, *others):
    return list(lax.optimization_barrier((tuple(xs), others))[0])


def body(features, blocks, codes, counts, weight, bias):
    block = blocks.shape[-1]
    size = features.shape[0]
    where = jnp.stack([lax.axis_index("row"), lax.axis_index("rep")]).astype(jnp.int32)
    blocks = blocks.reshape(blocks.shape[2:])
    codes = jnp.concatenate([codes.reshape(codes.shape[2:]).T, counts.reshape(1, -1)])
    other_codes = send(codes, "C")
    held = {HOME: (features, 0)}
    arrays = [(features, (HOME,))]

    def payload(units):
        for x, us in arrays:
            if set(us) == set(units):
                return x, us
        x = [held[u][0][held[u][1] * size : (held[u][1] + 1) * size] for u in units]
        return x[0] if len(x) == 1 else jnp.concatenate(x), units

    def exchange(number, payloads, late, first, second):
        group = []
        payloads = [p for p in payloads if p[0] not in late] + [p for p in payloads if p[0] in late]
        for channel, x, units in payloads:
            x = after([x], *first, *(second if channel in late else ()))[0] if first else x
            x, units = send(x, channel), tuple(arrived(channel, u) for u in units)
            for at, u in enumerate(units):
                assert u not in held, u
                held[u] = (x, at)
            group.append((x, units))
        arrays.extend(group)
        return group

    def names(group):
        return tuple(u for _, us in group for u in us)

    def hold(group, *others):
        return [(x, us) for x, (_, us) in zip(after([x for x, _ in group], *others), group)]

    def payloads(number):
        return [(c,) + payload(us) for c, us in ROUNDS[number]]

    def xs(group):
        return [x for x, _ in group]

    def add(group, packed, running, half=None):
        return terms(group, packed, running, where, codes, blocks, half)

    group = exchange(0, payloads(0), (), (), ())

    moves = payloads(1)
    early, have = [], set()
    for x, us in [(features, (HOME,))] + [(x, us) for _, x, us in moves] + group:
        if not have & set(us):
            early.append((x, us))
            have |= set(us)
    group = exchange(1, moves, (), [*xs(group), other_codes], ())
    blocks = load(blocks)
    count = len(names(early)) + len(names(group))
    packed = pack(early, where, other_codes, block, count)

    moves = payloads(2)
    group = hold(group, packed, blocks)
    packed = pack(group, where, other_codes, block, count, packed)
    first = xs(group) + [packed]
    ready = early + group
    packed = [(send(packed, "C"), names(ready))]
    group = exchange(2, moves, LATE[2], first, xs(packed))
    running = add(ready, packed, None)

    moves = payloads(3)
    group = hold(group, running)
    packed = pack(group, where, other_codes, block, len(names(group)))
    first = xs(group) + [packed]
    ready = group
    packed = [(send(packed, "C"), names(group))]
    group = exchange(3, moves, LATE[3], first, xs(packed))
    running = add(ready, packed, running)

    group = hold(group, running)
    packed = pack(group, where, other_codes, block, len(names(group)))
    packed = [(send(packed, "C"), names(group))]
    sent = add(group, [], running, 1)
    sent = add([], packed, sent, 1)
    kept = add(group, packed, running, 0)
    received = lax.ppermute(sent.astype(jnp.bfloat16), "rep", [(0, 1), (1, 0)])
    shares = (kept + received.astype(jnp.float32)).astype(jnp.bfloat16)
    hidden = jnp.dot(shares, weight, preferred_element_type=jnp.float32) + bias
    return jnp.maximum(hidden, 0.0).astype(jnp.bfloat16)


def solution(mesh):
    placed = (
        P(("row", "rep"), None),
        P("row", "rep", None, None, None, None),
        P("row", "rep", None, None),
        P("row", "rep", None),
        P(),
        P(),
    )
    return jax.shard_map(
        body, mesh=mesh, in_specs=placed, out_specs=P(("row", "rep"), None), check_vma=False
    )
```

profile of v0, /device:TPU:1, one launch (start us, length us, event | category | flops | bytes accessed | tf_op | source)
XLA Modules:
  0.0 85.4 jit_solution(12938086100033984924)
XLA Ops:
  0.0 2.5 %collective-permute-start = (bf16[1024,128]{1,0:T(8,128)(2,1)}, bf16[1024,128]{1,0:T(8,128)(2,1)S(1)}, u32[]{:S(2)}, u32[]{:S(2)}) collective-permute-start(bf16[1024,128]{1,0:T(8,128)(2,1)} %refs_0_.3), channel_id=1, source_target_pairs={{0,48},{1,17},{2,14},{3,7},{4,52},{5,21},{6,2},{7,11},{8,56},{9,25... | collective-permute-start | bytes 786440 | tf_op jit(solution)/shard_map/ppermute | solution.py:75
  2.5 1.3 %collective-permute-start.1 = (bf16[1024,128]{1,0:T(8,128)(2,1)}, bf16[1024,128]{1,0:T(8,128)(2,1)S(1)}, u32[]{:S(2)}, u32[]{:S(2)}) collective-permute-start(bf16[1024,128]{1,0:T(8,128)(2,1)} %refs_0_.3), channel_id=1, source_target_pairs={{0,12},{1,5},{2,50},{3,19},{4,0},{5,9},{6,54},{7,23},{8,4},{9,13},... | collective-permute-start | bytes 786440 | tf_op jit(solution)/shard_map/ppermute | solution.py:75
  3.8 2.7 %collective-permute-start.3 = (bf16[1024,128]{1,0:T(8,128)(2,1)}, bf16[1024,128]{1,0:T(8,128)(2,1)S(1)}, u32[]{:S(2)}, u32[]{:S(2)}) collective-permute-start(bf16[1024,128]{1,0:T(8,128)(2,1)} %refs_0_.3), channel_id=1, source_target_pairs={{0,2},{1,3},{2,0},{3,1},{4,6},{5,7},{6,4},{7,5},{8,10},{9,11},{10,... | collective-permute-start | bytes 786440 | tf_op jit(solution)/shard_map/ppermute | solution.py:75
  6.5 2.1 %collective-permute-start.2 = (bf16[1024,128]{1,0:T(8,128)(2,1)}, bf16[1024,128]{1,0:T(8,128)(2,1)S(1)}, u32[]{:S(2)}, u32[]{:S(2)}) collective-permute-start(bf16[1024,128]{1,0:T(8,128)(2,1)} %refs_0_.3), channel_id=1, source_target_pairs={{0,16},{1,49},{2,6},{3,15},{4,20},{5,53},{6,10},{7,3},{8,24},{9,57... | collective-permute-start | bytes 786440 | tf_op jit(solution)/shard_map/ppermute | solution.py:75
  8.6 1.6 %collective-permute-start.4 = (bf16[1024,128]{1,0:T(8,128)(2,1)}, bf16[1024,128]{1,0:T(8,128)(2,1)S(1)}, u32[]{:S(2)}, u32[]{:S(2)}) collective-permute-start(bf16[1024,128]{1,0:T(8,128)(2,1)} %refs_0_.3), channel_id=1, source_target_pairs={{0,4},{1,13},{2,18},{3,51},{4,8},{5,1},{6,22},{7,55},{8,12},{9,5},... | collective-permute-start | bytes 786440 | tf_op jit(solution)/shard_map/ppermute | solution.py:75
  10.9 1.4 %collective-permute-start.5 = (s32[3,64]{1,0:T(4,128)S(1)}, s32[3,64]{1,0:T(4,128)S(1)}, u32[]{:S(2)}, u32[]{:S(2)}) collective-permute-start(s32[3,64]{1,0:T(4,128)S(1)} %pad_add_fusion.codes), channel_id=1, source_target_pairs={{0,1},{1,0},{2,3},{3,2},{4,5},{5,4},{6,7},{7,6},{8,9},{9,8},{10,11... | collective-permute-start | bytes 2312 | tf_op jit(solution)/shard_map/ppermute | solution.py:75
  13.4 1.7 %collective-permute-done.4 = bf16[1024,128]{1,0:T(8,128)(2,1)S(1)} collective-permute-done((bf16[1024,128]{1,0:T(8,128)(2,1)}, bf16[1024,128]{1,0:T(8,128)(2,1)S(1)}, u32[]{:S(2)}, u32[]{:S(2)}) %collective-permute-start.4) | collective-permute-done | bytes 262176 | tf_op jit(solution)/shard_map/ppermute | solution.py:75
  16.4 2.9 %collective-permute-start.8 = (bf16[2048,128]{1,0:T(8,128)(2,1)S(1)}, bf16[2048,128]{1,0:T(8,128)(2,1)S(1)}, u32[]{:S(2)}, u32[]{:S(2)}) collective-permute-start(bf16[2048,128]{1,0:T(8,128)(2,1)S(1)} %constant_dynamic-update-slice_fusion.refs_1_), channel_id=1, source_target_pairs={{0,2},{1,3},{2,0},{3,1},{4,6},{5,7},{6,4},{7,5},{8,10},{9,11},{10,... | collective-permute-start | bytes 1572872 | tf_op jit(solution)/shard_map/ppermute | solution.py:75
  19.3 1.6 %collective-permute-start.9 = (bf16[2048,128]{1,0:T(8,128)(2,1)S(1)}, bf16[2048,128]{1,0:T(8,128)(2,1)S(1)}, u32[]{:S(2)}, u32[]{:S(2)}) collective-permute-start(bf16[2048,128]{1,0:T(8,128)(2,1)S(1)} %constant_dynamic-update-slice_fusion.2.refs_2_), channel_id=1, source_target_pairs={{0,4},{1,13},{2,18},{3,51},{4,8},{5,1},{6,22},{7,55},{8,12},{9,5},... | collective-permute-start | bytes 1572872 | tf_op jit(solution)/shard_map/ppermute | solution.py:75
  20.9 1.2 %collective-permute-start.7 = (bf16[2048,128]{1,0:T(8,128)(2,1)S(1)}, bf16[2048,128]{1,0:T(8,128)(2,1)}, u32[]{:S(2)}, u32[]{:S(2)}) collective-permute-start(bf16[2048,128]{1,0:T(8,128)(2,1)S(1)} %constant_dynamic-update-slice_fusion.refs_1_), channel_id=1, source_target_pairs={{0,16},{1,49},{2,6},{3,15},{4,20},{5,53},{6,10},{7,3},{8,24},{9,57... | collective-permute-start | bytes 1572872 | tf_op jit(solution)/shard_map/ppermute | solution.py:75
  22.2 5.8 %load.1.blocks = bf16[64,2,256,256]{3,2,1,0:T(8,128)(2,1)S(1)} custom-call(bf16[64,2,256,256]{3,2,1,0:T(8,128)(2,1)} %bitcast.8), custom_call_target="tpu_custom_call" | custom-call | bytes 16777216 | tf_op jit(solution)/shard_map/load/pallas_call | solution.py:248
  28.9 3.9 %collective-permute-done.9.refs_3_.refs_7_ = bf16[2048,128]{1,0:T(8,128)(2,1)S(1)} collective-permute-done((bf16[2048,128]{1,0:T(8,128)(2,1)S(1)}, bf16[2048,128]{1,0:T(8,128)(2,1)S(1)}, u32[]{:S(2)}, u32[]{:S(2)}) %collective-permute-start.9) | collective-permute-done | bytes 524320 | tf_op jit(solution)/shard_map/ppermute | solution.py:75
  32.8 2.1 %collective-permute-done.7.refs_0_.refs_4_ = bf16[2048,128]{1,0:T(8,128)(2,1)} collective-permute-done((bf16[2048,128]{1,0:T(8,128)(2,1)S(1)}, bf16[2048,128]{1,0:T(8,128)(2,1)}, u32[]{:S(2)}, u32[]{:S(2)}) %collective-permute-start.7) | collective-permute-done | bytes 524320 | tf_op jit(solution)/shard_map/ppermute | solution.py:75
  34.8 1.4 %pack.5 = bf16[32,256,128]{2,1,0:T(8,128)(2,1)S(1)} custom-call(s32[2]{0:T(128)S(1)} %pad_add_fusion.1.where, s32[3,64]{1,0:T(4,128)S(1)} %collective-permute-done.5.codes, bf16[2048,128]{1,0:T(8,128)(2,1)} %collective-permute-done.7.refs_0_.refs_4_, bf16[2048,128]{1,0:T(8,128)(2,1)S(1)} %collective-permute-done.6.refs_1_.refs_5_, ...), custom_call_target="tpu_custom_call", output_to_operand_aliasing={{}: (7, {})} | custom-call | bytes 2621440 | tf_op jit(solution)/shard_map/pack/pallas_call | solution.py:113
  36.2 1.7 %collective-permute-start.14 = (bf16[32,256,128]{2,1,0:T(8,128)(2,1)S(1)}, bf16[32,256,128]{2,1,0:T(8,128)(2,1)S(1)}, u32[]{:S(2)}, u32[]{:S(2)}) collective-permute-start(bf16[32,256,128]{2,1,0:T(8,128)(2,1)S(1)} %pack.5), channel_id=1, source_target_pairs={{0,1},{1,0},{2,3},{3,2},{4,5},{5,4},{6,7},{7,6},{8,9},{9,8},{10,11... | collective-permute-start | bytes 6291464 | tf_op jit(solution)/shard_map/ppermute | solution.py:75
  37.9 1.2 %collective-permute-start.11 = (bf16[2048,128]{1,0:T(8,128)(2,1)S(1)}, bf16[2048,128]{1,0:T(8,128)(2,1)S(1)}, u32[]{:S(2)}, u32[]{:S(2)}) collective-permute-start(bf16[2048,128]{1,0:T(8,128)(2,1)S(1)} %collective-permute-done.6.refs_1_.refs_5_), channel_id=1, source_target_pairs={{0,2},{1,3},{2,0},{3,1},{4,6},{5,7},{6,4},{7,5},{8,10},{9,11},{10,... | collective-permute-start | bytes 1572872 | tf_op jit(solution)/shard_map/ppermute | solution.py:75
  39.2 1.6 %collective-permute-start.13 = (bf16[2048,128]{1,0:T(8,128)(2,1)S(1)}, bf16[2048,128]{1,0:T(8,128)(2,1)S(1)}, u32[]{:S(2)}, u32[]{:S(2)}) collective-permute-start(bf16[2048,128]{1,0:T(8,128)(2,1)S(1)} %collective-permute-done.6.refs_1_.refs_5_), channel_id=1, source_target_pairs={{0,12},{1,5},{2,50},{3,19},{4,0},{5,9},{6,54},{7,23},{8,4},{9,13},... | collective-permute-start | bytes 1572872 | tf_op jit(solution)/shard_map/ppermute | solution.py:75
  41.7 1.3 %collective-permute-start.16 = (bf16[2048,128]{1,0:T(8,128)(2,1)S(1)}, bf16[2048,128]{1,0:T(8,128)(2,1)S(1)}, u32[]{:S(2)}, u32[]{:S(2)}) collective-permute-start(bf16[2048,128]{1,0:T(8,128)(2,1)S(1)} %collective-permute-done.8.refs_2_.refs_6_), channel_id=1, source_target_pairs={{0,4},{1,13},{2,18},{3,51},{4,8},{5,1},{6,22},{7,55},{8,12},{9,5},... | collective-permute-start | bytes 1572872 | tf_op jit(solution)/shard_map/ppermute | solution.py:75
  43.1 2.0 %collective-permute-start.15 = (bf16[2048,128]{1,0:T(8,128)(2,1)S(1)}, bf16[2048,128]{1,0:T(8,128)(2,1)S(1)}, u32[]{:S(2)}, u32[]{:S(2)}) collective-permute-start(bf16[2048,128]{1,0:T(8,128)(2,1)S(1)} %collective-permute-done.10.refs_4_.refs_8_), channel_id=1, source_target_pairs={{0,16},{1,49},{2,6},{3,15},{4,20},{5,53},{6,10},{7,3},{8,24},{9,57... | collective-permute-start | bytes 1572872 | tf_op jit(solution)/shard_map/ppermute | solution.py:75
  45.0 8.1 %terms.5.refs_6_ = f32[2048,128]{1,0:T(8,128)S(1)} custom-call(s32[2]{0:T(128)S(1)} %pad_add_fusion.1.where, s32[3,64]{1,0:T(4,128)S(1)} %pad_add_fusion.codes, bf16[64,2,256,256]{3,2,1,0:T(8,128)(2,1)S(1)} %load.1.blocks, bf16[1024,128]{1,0:T(8,128)(2,1)S(1)} %copy-done.1, bf16[2048,128]{1,0:T(8,128)(2,1)S(1)} %constant_dynamic-update-slice_fusion.refs_1_, ...), custom_call_target="tpu_custom_call" | custom-call | flops 1073741824 | bytes 12582912 | tf_op jit(solution)/shard_map/terms/pallas_call | solution.py:225
  53.9 2.1 %collective-permute-done.15.refs_3_ = bf16[2048,128]{1,0:T(8,128)(2,1)S(1)} collective-permute-done((bf16[2048,128]{1,0:T(8,128)(2,1)S(1)}, bf16[2048,128]{1,0:T(8,128)(2,1)S(1)}, u32[]{:S(2)}, u32[]{:S(2)}) %collective-permute-start.15) | collective-permute-done | bytes 524320 | tf_op jit(solution)/shard_map/ppermute | solution.py:75
  57.5 1.5 %collective-permute-start.20 = (bf16[2048,128]{1,0:T(8,128)(2,1)S(1)}, bf16[2048,128]{1,0:T(8,128)(2,1)S(1)}, u32[]{:S(2)}, u32[]{:S(2)}) collective-permute-start(bf16[2048,128]{1,0:T(8,128)(2,1)S(1)} %collective-permute-done.12.refs_0_), channel_id=1, source_target_pairs={{0,4},{1,13},{2,18},{3,51},{4,8},{5,1},{6,22},{7,55},{8,12},{9,5},... | collective-permute-start | bytes 1572872 | tf_op jit(solution)/shard_map/ppermute | solution.py:75
  59.4 1.2 %collective-permute-start.18 = (bf16[1024,128]{1,0:T(8,128)(2,1)S(1)}, bf16[1024,128]{1,0:T(8,128)(2,1)S(1)}, u32[]{:S(2)}, u32[]{:S(2)}) collective-permute-start(bf16[1024,128]{1,0:T(8,128)(2,1)S(1)} %slice.21), channel_id=1, source_target_pairs={{0,16},{1,49},{2,6},{3,15},{4,20},{5,53},{6,10},{7,3},{8,24},{9,57... | collective-permute-start | bytes 786440 | tf_op jit(solution)/shard_map/ppermute | solution.py:75
  60.6 1.5 %collective-permute-start.19 = (bf16[1024,128]{1,0:T(8,128)(2,1)S(1)}, bf16[1024,128]{1,0:T(8,128)(2,1)S(1)}, u32[]{:S(2)}, u32[]{:S(2)}) collective-permute-start(bf16[1024,128]{1,0:T(8,128)(2,1)S(1)} %slice.24), channel_id=1, source_target_pairs={{0,2},{1,3},{2,0},{3,1},{4,6},{5,7},{6,4},{7,5},{8,10},{9,11},{10,... | collective-permute-start | bytes 786440 | tf_op jit(solution)/shard_map/ppermute | solution.py:75
  62.1 4.4 %terms.6.refs_6_.refs_5_ = f32[2048,128]{1,0:T(8,128)S(1)} custom-call(s32[2]{0:T(128)S(1)} %pad_add_fusion.1.where, s32[3,64]{1,0:T(4,128)S(1)} %pad_add_fusion.codes, bf16[64,2,256,256]{3,2,1,0:T(8,128)(2,1)S(1)} %load.1.blocks, bf16[2048,128]{1,0:T(8,128)(2,1)S(1)} %collective-permute-done.12.refs_0_, ...), custom_call_target="tpu_custom_call" | custom-call | flops 671088640 | bytes 7864320 | tf_op jit(solution)/shard_map/terms/pallas_call | solution.py:225
  67.6 1.3 %collective-permute-done.17.refs_0_ = bf16[1024,128]{1,0:T(8,128)(2,1)S(1)} collective-permute-done((bf16[1024,128]{1,0:T(8,128)(2,1)S(1)}, bf16[1024,128]{1,0:T(8,128)(2,1)S(1)}, u32[]{:S(2)}, u32[]{:S(2)}) %collective-permute-start.17) | collective-permute-done | bytes 262176 | tf_op jit(solution)/shard_map/ppermute | solution.py:75
  68.9 1.9 %collective-permute-done.18.refs_1_ = bf16[1024,128]{1,0:T(8,128)(2,1)S(1)} collective-permute-done((bf16[1024,128]{1,0:T(8,128)(2,1)S(1)}, bf16[1024,128]{1,0:T(8,128)(2,1)S(1)}, u32[]{:S(2)}, u32[]{:S(2)}) %collective-permute-start.18) | collective-permute-done | bytes 262176 | tf_op jit(solution)/shard_map/ppermute | solution.py:75
  71.6 1.4 %collective-permute-start.23 = (bf16[12,256,128]{2,1,0:T(8,128)(2,1)S(1)}, bf16[12,256,128]{2,1,0:T(8,128)(2,1)S(1)}, u32[]{:S(2)}, u32[]{:S(2)}) collective-permute-start(bf16[12,256,128]{2,1,0:T(8,128)(2,1)S(1)} %pack.7), channel_id=1, source_target_pairs={{0,1},{1,0},{2,3},{3,2},{4,5},{5,4},{6,7},{7,6},{8,9},{9,8},{10,11... | collective-permute-start | bytes 2359304 | tf_op jit(solution)/shard_map/ppermute | solution.py:75
  73.0 1.7 %terms.8.refs_1_ = f32[1024,128]{1,0:T(8,128)S(1)} custom-call(s32[2]{0:T(128)S(1)} %pad_add_fusion.1.where, s32[3,64]{1,0:T(4,128)S(1)} %pad_add_fusion.codes, bf16[64,2,256,256]{3,2,1,0:T(8,128)(2,1)S(1)} %load.1.blocks, bf16[1024,128]{1,0:T(8,128)(2,1)S(1)} %collective-permute-done.17.refs_0_, bf16[1024,128]{1,0:T(8,128)(2,1)S(1)} %collective-permute-done.18.refs_1_, ...), custom_call_target="tpu_custom_call" | custom-call | flops 201326592 | bytes 2359296 | tf_op jit(solution)/shard_map/terms/pallas_call | solution.py:225
  74.9 1.4 %terms.9 = f32[1024,128]{1,0:T(8,128)S(1)} custom-call(s32[2]{0:T(128)S(1)} %pad_add_fusion.1.where, s32[3,64]{1,0:T(4,128)S(1)} %pad_add_fusion.codes, bf16[64,2,256,256]{3,2,1,0:T(8,128)(2,1)S(1)} %load.1.blocks, bf16[12,256,128]{2,1,0:T(8,128)(2,1)S(1)} %collective-permute-done.23.refs_5_.refs_0_, f32[1024,128]{1,0:T(8,128)S(1)} %terms.8.refs_1_), custom_call_target="tpu_custom_call" | custom-call | flops 201326592 | bytes 2359296 | tf_op jit(solution)/shard_map/terms/pallas_call | solution.py:225
  76.5 2.1 %terms.7 = f32[1024,128]{1,0:T(8,128)S(1)} custom-call(s32[2]{0:T(128)S(1)} %pad_add_fusion.1.where, s32[3,64]{1,0:T(4,128)S(1)} %pad_add_fusion.codes, bf16[64,2,256,256]{3,2,1,0:T(8,128)(2,1)S(1)} %load.1.blocks, bf16[1024,128]{1,0:T(8,128)(2,1)S(1)} %collective-permute-done.17.refs_0_, bf16[1024,128]{1,0:T(8,128)(2,1)S(1)} %collective-permute-done.18.refs_1_, ...), custom_call_target="tpu_custom_call" | custom-call | flops 402653184 | bytes 4718592 | tf_op jit(solution)/shard_map/terms/pallas_call | solution.py:225
  78.5 5.8 %collective-permute-done.24 = bf16[1024,128]{1,0:T(8,128)(2,1)S(1)} collective-permute-done((bf16[1024,128]{1,0:T(8,128)(2,1)S(1)}, bf16[1024,128]{1,0:T(8,128)(2,1)S(1)}, u32[]{:S(2)}, u32[]{:S(2)}) %collective-permute-start.24) | collective-permute-done | bytes 262176 | tf_op jit(solution)/shard_map/ppermute | solution.py:346
  (49 shorter events, 10.6 us)
Async XLA Ops:
  0.0 84.3 %copy-start = (bf16[128,256]{1,0:T(8,128)(2,1)S(1)}, bf16[128,256]{1,0:T(8,128)(2,1)}, u32[]{:S(2)}) copy-start(bf16[128,256]{1,0:T(8,128)(2,1)} %param.10) | copy-start | bytes 196612
  0.0 10.9 %collective-permute-start = (bf16[1024,128]{1,0:T(8,128)(2,1)}, bf16[1024,128]{1,0:T(8,128)(2,1)S(1)}, u32[]{:S(2)}, u32[]{:S(2)}) collective-permute-start(bf16[1024,128]{1,0:T(8,128)(2,1)} %refs_0_.3), channel_id=1, source_target_pairs={{0,48},{1,17},{2,14},{3,7},{4,52},{5,21},{6,2},{7,11},{8,56},{9,25... | collective-permute-start | bytes 786440 | tf_op jit(solution)/shard_map/ppermute | solution.py:75
  2.5 9.9 %collective-permute-start.1 = (bf16[1024,128]{1,0:T(8,128)(2,1)}, bf16[1024,128]{1,0:T(8,128)(2,1)S(1)}, u32[]{:S(2)}, u32[]{:S(2)}) collective-permute-start(bf16[1024,128]{1,0:T(8,128)(2,1)} %refs_0_.3), channel_id=1, source_target_pairs={{0,12},{1,5},{2,50},{3,19},{4,0},{5,9},{6,54},{7,23},{8,4},{9,13},... | collective-permute-start | bytes 786440 | tf_op jit(solution)/shard_map/ppermute | solution.py:75
  3.8 8.6 %collective-permute-start.3 = (bf16[1024,128]{1,0:T(8,128)(2,1)}, bf16[1024,128]{1,0:T(8,128)(2,1)S(1)}, u32[]{:S(2)}, u32[]{:S(2)}) collective-permute-start(bf16[1024,128]{1,0:T(8,128)(2,1)} %refs_0_.3), channel_id=1, source_target_pairs={{0,2},{1,3},{2,0},{3,1},{4,6},{5,7},{6,4},{7,5},{8,10},{9,11},{10,... | collective-permute-start | bytes 786440 | tf_op jit(solution)/shard_map/ppermute | solution.py:75
  6.5 6.9 %collective-permute-start.2 = (bf16[1024,128]{1,0:T(8,128)(2,1)}, bf16[1024,128]{1,0:T(8,128)(2,1)S(1)}, u32[]{:S(2)}, u32[]{:S(2)}) collective-permute-start(bf16[1024,128]{1,0:T(8,128)(2,1)} %refs_0_.3), channel_id=1, source_target_pairs={{0,16},{1,49},{2,6},{3,15},{4,20},{5,53},{6,10},{7,3},{8,24},{9,57... | collective-permute-start | bytes 786440 | tf_op jit(solution)/shard_map/ppermute | solution.py:75
  8.6 6.5 %collective-permute-start.4 = (bf16[1024,128]{1,0:T(8,128)(2,1)}, bf16[1024,128]{1,0:T(8,128)(2,1)S(1)}, u32[]{:S(2)}, u32[]{:S(2)}) collective-permute-start(bf16[1024,128]{1,0:T(8,128)(2,1)} %refs_0_.3), channel_id=1, source_target_pairs={{0,4},{1,13},{2,18},{3,51},{4,8},{5,1},{6,22},{7,55},{8,12},{9,5},... | collective-permute-start | bytes 786440 | tf_op jit(solution)/shard_map/ppermute | solution.py:75
  10.9 2.5 %collective-permute-start.5 = (s32[3,64]{1,0:T(4,128)S(1)}, s32[3,64]{1,0:T(4,128)S(1)}, u32[]{:S(2)}, u32[]{:S(2)}) collective-permute-start(s32[3,64]{1,0:T(4,128)S(1)} %pad_add_fusion.codes), channel_id=1, source_target_pairs={{0,1},{1,0},{2,3},{3,2},{4,5},{5,4},{6,7},{7,6},{8,9},{9,8},{10,11... | collective-permute-start | bytes 2312 | tf_op jit(solution)/shard_map/ppermute | solution.py:75
  15.2 13.6 %collective-permute-start.10 = (bf16[2048,128]{1,0:T(8,128)(2,1)}, bf16[2048,128]{1,0:T(8,128)(2,1)S(1)}, u32[]{:S(2)}, u32[]{:S(2)}) collective-permute-start(bf16[2048,128]{1,0:T(8,128)(2,1)} %get-tuple-element.35), channel_id=1, source_target_pairs={{0,12},{1,5},{2,50},{3,19},{4,0},{5,9},{6,54},{7,23},{8,4},{9,13},... | collective-permute-start | bytes 1572872 | tf_op jit(solution)/shard_map/ppermute | solution.py:75
  15.8 13.0 %collective-permute-start.6 = (bf16[2048,128]{1,0:T(8,128)(2,1)}, bf16[2048,128]{1,0:T(8,128)(2,1)S(1)}, u32[]{:S(2)}, u32[]{:S(2)}) collective-permute-start(bf16[2048,128]{1,0:T(8,128)(2,1)} %get-tuple-element.32), channel_id=1, source_target_pairs={{0,48},{1,17},{2,14},{3,7},{4,52},{5,21},{6,2},{7,11},{8,56},{9,25... | collective-permute-start | bytes 1572872 | tf_op jit(solution)/shard_map/ppermute | solution.py:75
  16.4 12.5 %collective-permute-start.8 = (bf16[2048,128]{1,0:T(8,128)(2,1)S(1)}, bf16[2048,128]{1,0:T(8,128)(2,1)S(1)}, u32[]{:S(2)}, u32[]{:S(2)}) collective-permute-start(bf16[2048,128]{1,0:T(8,128)(2,1)S(1)} %constant_dynamic-update-slice_fusion.refs_1_), channel_id=1, source_target_pairs={{0,2},{1,3},{2,0},{3,1},{4,6},{5,7},{6,4},{7,5},{8,10},{9,11},{10,... | collective-permute-start | bytes 1572872 | tf_op jit(solution)/shard_map/ppermute | solution.py:75
  19.3 13.5 %collective-permute-start.9 = (bf16[2048,128]{1,0:T(8,128)(2,1)S(1)}, bf16[2048,128]{1,0:T(8,128)(2,1)S(1)}, u32[]{:S(2)}, u32[]{:S(2)}) collective-permute-start(bf16[2048,128]{1,0:T(8,128)(2,1)S(1)} %constant_dynamic-update-slice_fusion.2.refs_2_), channel_id=1, source_target_pairs={{0,4},{1,13},{2,18},{3,51},{4,8},{5,1},{6,22},{7,55},{8,12},{9,5},... | collective-permute-start | bytes 1572872 | tf_op jit(solution)/shard_map/ppermute | solution.py:75
  20.9 13.9 %collective-permute-start.7 = (bf16[2048,128]{1,0:T(8,128)(2,1)S(1)}, bf16[2048,128]{1,0:T(8,128)(2,1)}, u32[]{:S(2)}, u32[]{:S(2)}) collective-permute-start(bf16[2048,128]{1,0:T(8,128)(2,1)S(1)} %constant_dynamic-update-slice_fusion.refs_1_), channel_id=1, source_target_pairs={{0,16},{1,49},{2,6},{3,15},{4,20},{5,53},{6,10},{7,3},{8,24},{9,57... | collective-permute-start | bytes 1572872 | tf_op jit(solution)/shard_map/ppermute | solution.py:75
  22.2 5.9 %copy-start.1 = (bf16[1024,128]{1,0:T(8,128)(2,1)S(1)}, bf16[1024,128]{1,0:T(8,128)(2,1)}, u32[]{:S(2)}) copy-start(bf16[1024,128]{1,0:T(8,128)(2,1)} %refs_0_.3) | copy-start | bytes 786436
  36.2 5.5 %collective-permute-start.14 = (bf16[32,256,128]{2,1,0:T(8,128)(2,1)S(1)}, bf16[32,256,128]{2,1,0:T(8,128)(2,1)S(1)}, u32[]{:S(2)}, u32[]{:S(2)}) collective-permute-start(bf16[32,256,128]{2,1,0:T(8,128)(2,1)S(1)} %pack.5), channel_id=1, source_target_pairs={{0,1},{1,0},{2,3},{3,2},{4,5},{5,4},{6,7},{7,6},{8,9},{9,8},{10,11... | collective-permute-start | bytes 6291464 | tf_op jit(solution)/shard_map/ppermute | solution.py:75
  37.9 15.2 %collective-permute-start.11 = (bf16[2048,128]{1,0:T(8,128)(2,1)S(1)}, bf16[2048,128]{1,0:T(8,128)(2,1)S(1)}, u32[]{:S(2)}, u32[]{:S(2)}) collective-permute-start(bf16[2048,128]{1,0:T(8,128)(2,1)S(1)} %collective-permute-done.6.refs_1_.refs_5_), channel_id=1, source_target_pairs={{0,2},{1,3},{2,0},{3,1},{4,6},{5,7},{6,4},{7,5},{8,10},{9,11},{10,... | collective-permute-start | bytes 1572872 | tf_op jit(solution)/shard_map/ppermute | solution.py:75
  39.2 14.0 %collective-permute-start.13 = (bf16[2048,128]{1,0:T(8,128)(2,1)S(1)}, bf16[2048,128]{1,0:T(8,128)(2,1)S(1)}, u32[]{:S(2)}, u32[]{:S(2)}) collective-permute-start(bf16[2048,128]{1,0:T(8,128)(2,1)S(1)} %collective-permute-done.6.refs_1_.refs_5_), channel_id=1, source_target_pairs={{0,12},{1,5},{2,50},{3,19},{4,0},{5,9},{6,54},{7,23},{8,4},{9,13},... | collective-permute-start | bytes 1572872 | tf_op jit(solution)/shard_map/ppermute | solution.py:75
  40.8 12.3 %collective-permute-start.12 = (bf16[2048,128]{1,0:T(8,128)(2,1)S(1)}, bf16[2048,128]{1,0:T(8,128)(2,1)S(1)}, u32[]{:S(2)}, u32[]{:S(2)}) collective-permute-start(bf16[2048,128]{1,0:T(8,128)(2,1)S(1)} %pad_maximum_fusion.2), channel_id=1, source_target_pairs={{0,48},{1,17},{2,14},{3,7},{4,52},{5,21},{6,2},{7,11},{8,56},{9,25... | collective-permute-start | bytes 1572872 | tf_op jit(solution)/shard_map/ppermute | solution.py:75
  41.7 12.2 %collective-permute-start.16 = (bf16[2048,128]{1,0:T(8,128)(2,1)S(1)}, bf16[2048,128]{1,0:T(8,128)(2,1)S(1)}, u32[]{:S(2)}, u32[]{:S(2)}) collective-permute-start(bf16[2048,128]{1,0:T(8,128)(2,1)S(1)} %collective-permute-done.8.refs_2_.refs_6_), channel_id=1, source_target_pairs={{0,4},{1,13},{2,18},{3,51},{4,8},{5,1},{6,22},{7,55},{8,12},{9,5},... | collective-permute-start | bytes 1572872 | tf_op jit(solution)/shard_map/ppermute | solution.py:75
  43.1 13.0 %collective-permute-start.15 = (bf16[2048,128]{1,0:T(8,128)(2,1)S(1)}, bf16[2048,128]{1,0:T(8,128)(2,1)S(1)}, u32[]{:S(2)}, u32[]{:S(2)}) collective-permute-start(bf16[2048,128]{1,0:T(8,128)(2,1)S(1)} %collective-permute-done.10.refs_4_.refs_8_), channel_id=1, source_target_pairs={{0,16},{1,49},{2,6},{3,15},{4,20},{5,53},{6,10},{7,3},{8,24},{9,57... | collective-permute-start | bytes 1572872 | tf_op jit(solution)/shard_map/ppermute | solution.py:75
  57.0 5.1 %collective-permute-start.21 = (bf16[20,256,128]{2,1,0:T(8,128)(2,1)S(1)}, bf16[20,256,128]{2,1,0:T(8,128)(2,1)S(1)}, u32[]{:S(2)}, u32[]{:S(2)}) collective-permute-start(bf16[20,256,128]{2,1,0:T(8,128)(2,1)S(1)} %pack.6), channel_id=1, source_target_pairs={{0,1},{1,0},{2,3},{3,2},{4,5},{5,4},{6,7},{7,6},{8,9},{9,8},{10,11... | collective-permute-start | bytes 3932168 | tf_op jit(solution)/shard_map/ppermute | solution.py:75
  57.5 13.4 %collective-permute-start.20 = (bf16[2048,128]{1,0:T(8,128)(2,1)S(1)}, bf16[2048,128]{1,0:T(8,128)(2,1)S(1)}, u32[]{:S(2)}, u32[]{:S(2)}) collective-permute-start(bf16[2048,128]{1,0:T(8,128)(2,1)S(1)} %collective-permute-done.12.refs_0_), channel_id=1, source_target_pairs={{0,4},{1,13},{2,18},{3,51},{4,8},{5,1},{6,22},{7,55},{8,12},{9,5},... | collective-permute-start | bytes 1572872 | tf_op jit(solution)/shard_map/ppermute | solution.py:75
  59.0 9.9 %collective-permute-start.17 = (bf16[1024,128]{1,0:T(8,128)(2,1)S(1)}, bf16[1024,128]{1,0:T(8,128)(2,1)S(1)}, u32[]{:S(2)}, u32[]{:S(2)}) collective-permute-start(bf16[1024,128]{1,0:T(8,128)(2,1)S(1)} %slice.21), channel_id=1, source_target_pairs={{0,32},{1,33},{2,10},{3,11},{4,36},{5,37},{6,14},{7,15},{8,40},{9,... | collective-permute-start | bytes 786440 | tf_op jit(solution)/shard_map/ppermute | solution.py:75
  59.4 11.4 %collective-permute-start.18 = (bf16[1024,128]{1,0:T(8,128)(2,1)S(1)}, bf16[1024,128]{1,0:T(8,128)(2,1)S(1)}, u32[]{:S(2)}, u32[]{:S(2)}) collective-permute-start(bf16[1024,128]{1,0:T(8,128)(2,1)S(1)} %slice.21), channel_id=1, source_target_pairs={{0,16},{1,49},{2,6},{3,15},{4,20},{5,53},{6,10},{7,3},{8,24},{9,57... | collective-permute-start | bytes 786440 | tf_op jit(solution)/shard_map/ppermute | solution.py:75
  60.6 7.0 %collective-permute-start.19 = (bf16[1024,128]{1,0:T(8,128)(2,1)S(1)}, bf16[1024,128]{1,0:T(8,128)(2,1)S(1)}, u32[]{:S(2)}, u32[]{:S(2)}) collective-permute-start(bf16[1024,128]{1,0:T(8,128)(2,1)S(1)} %slice.24), channel_id=1, source_target_pairs={{0,2},{1,3},{2,0},{3,1},{4,6},{5,7},{6,4},{7,5},{8,10},{9,11},{10,... | collective-permute-start | bytes 786440 | tf_op jit(solution)/shard_map/ppermute | solution.py:75
  62.1 8.7 %collective-permute-start.22 = (bf16[1024,128]{1,0:T(8,128)(2,1)S(1)}, bf16[1024,128]{1,0:T(8,128)(2,1)S(1)}, u32[]{:S(2)}, u32[]{:S(2)}) collective-permute-start(bf16[1024,128]{1,0:T(8,128)(2,1)S(1)} %slice.25), channel_id=1, source_target_pairs={{0,12},{1,5},{2,50},{3,19},{4,0},{5,9},{6,54},{7,23},{8,4},{9,13},... | collective-permute-start | bytes 786440 | tf_op jit(solution)/shard_map/ppermute | solution.py:75
  71.6 3.3 %collective-permute-start.23 = (bf16[12,256,128]{2,1,0:T(8,128)(2,1)S(1)}, bf16[12,256,128]{2,1,0:T(8,128)(2,1)S(1)}, u32[]{:S(2)}, u32[]{:S(2)}) collective-permute-start(bf16[12,256,128]{2,1,0:T(8,128)(2,1)S(1)} %pack.7), channel_id=1, source_target_pairs={{0,1},{1,0},{2,3},{3,2},{4,5},{5,4},{6,7},{7,6},{8,9},{9,8},{10,11... | collective-permute-start | bytes 2359304 | tf_op jit(solution)/shard_map/ppermute | solution.py:75
  76.3 8.0 %copy-start.2 = (f32[256]{0:T(256)S(1)}, f32[256]{0:T(256)}, u32[]{:S(2)}) copy-start(f32[256]{0:T(256)} %param.11) | copy-start | bytes 3076
  76.4 8.0 %collective-permute-start.24 = (bf16[1024,128]{1,0:T(8,128)(2,1)S(1)}, bf16[1024,128]{1,0:T(8,128)(2,1)S(1)}, u32[]{:S(2)}, u32[]{:S(2)}) collective-permute-start(bf16[1024,128]{1,0:T(8,128)(2,1)S(1)} %convert_element_type.12), channel_id=1, source_target_pairs={{0,64},{64,0},{1,65},{65,1},{2,66},{66,2},{3,67},{67,3},{4,68},{68... | collective-permute-start | bytes 786440 | tf_op jit(solution)/shard_map/ppermute | solution.py:346
where the time goes:
time: 85.3 us; the launch traced here: 85.4 us
  starting transfers between devices  33 us (39%)
  Pallas kernels  27.3 us (32%)
  waiting for transfers between devices  21.7 us (25%)
  other arithmetic  1.9 us (2%)
  matrix products  1.08 us (1%)
    ppermute x24, starting transfers between devices, send(): return lax.ppermute(x, 'row', pairs_of(channel))  32.9 us
    pallas_call x5, Pallas kernels, terms(): pl.pallas_call(functools.partial(terms_kernel, layout, half), out_shape=j...  17.7 us
    ppermute x24, waiting for transfers between devices, send(): return lax.ppermute(x, 'row', pairs_of(channel))  15.9 us
    pallas_call x1, Pallas kernels, load(): pl.pallas_call(load_kernel, out_shape=pltpu.VMEM(blocks.shape, blocks.dty...  5.82 us
    ppermute x1, waiting for transfers between devices, body(): received = lax.ppermute(sent.astype(jnp.bfloat16), 'rep', [(0, 1), (1, 0)])  5.8 us
    pallas_call x4, Pallas kernels, pack(): pl.pallas_call(functools.partial(pack_kernel, layout, 0 if into is None e...  3.75 us
  transfers between devices with their start and end apart: 25, of which 11 were waited for; matrix products, arithmetic and copies ran while one was open for 2% of the time, Pallas kernels for 27%

commit v1 on v0

--- a/solution.py
+++ b/solution.py
@@ -11,36 +11,41 @@
 DIMS = (4, 4, 2, 2)
 SLOTS = 2
 VMEM_LIMIT = 4 * 2**20
-WIDTH = (2, 4)
 
 HOME = (0, 0, 0)
 ROUNDS = (
-    (("P1", (HOME,)), ("M1", (HOME,)), ("X", (HOME,)), ("P2", (HOME,)), ("M2", (HOME,))),
     (
-        ("P1", ((0, 0, 3), (0, 0, 1))),
-        ("M1", ((0, 1, 0), (0, 0, 1))),
-        ("X", ((0, 0, 3), (0, 0, 1))),
-        ("P2", ((1, 0, 0), (0, 1, 0))),
-        ("M2", ((1, 0, 0), (0, 0, 1))),
+        ("P2", (HOME,)),
+        ("M1", (HOME,)),
+        ("P1", (HOME,)),
+        ("X", (HOME,)),
+        ("M2", (HOME,)),
     ),
     (
-        ("P1", ((1, 0, 1), (0, 0, 2))),
-        ("M1", ((0, 1, 3), (1, 1, 0))),
-        ("X", ((0, 2, 0), (0, 1, 1))),
-        ("P2", ((1, 3, 0), (1, 1, 0))),
-        ("M2", ((0, 2, 0), (0, 1, 1))),
+        ("M1", ((1, 0, 0), (0, 0, 3))),
+        ("X", ((0, 0, 3), (0, 1, 0))),
+        ("P2", ((0, 3, 0), (1, 0, 0))),
+        ("P1", ((0, 0, 1), (0, 3, 0))),
+        ("M2", ((0, 1, 0), (0, 0, 1))),
     ),
     (
+        ("M2", ((1, 3, 0), (1, 0, 1))),
+        ("P2", ((0, 3, 3), (0, 1, 3))),
+        ("X", ((0, 0, 2), (0, 1, 1))),
+        ("M1", ((0, 1, 1), (1, 0, 3))),
+        ("P1", ((0, 3, 3), (1, 0, 3))),
+    ),
+    (
+        ("M1", ((0, 1, 2),)),
+        ("M2", ((1, 2, 0), (1, 3, 1))),
+        ("X", ((0, 2, 1),)),
         ("D1", ((1, 0, 2),)),
-        ("P1", ((1, 0, 2),)),
-        ("X", ((0, 2, 1),)),
-        ("P2", ((0, 2, 3), (1, 2, 0))),
-        ("M2", ((1, 2, 0),)),
+        ("P2", ((1, 2, 0),)),
     ),
 )
-MIRROR = True
-LATE = ((), (), ('P1', 'P2'), ('M2',))
-STEPS = {"P1": (0, 1), "M1": (0, -1), "D1": (0, 2), "P2": (1, 1), "M2": (1, -1)}
+LATE = ((), (), ("P1", "P2"), ("P2",))
+WIDTH = (2, 4)
+STEPS = {"P1": (0, 1), "M1": (0, -1), "D1": (0, 2), "D2": (1, 2), "P2": (1, 1), "M2": (1, -1)}
 
 
 def row_of(place):
@@ -58,7 +63,7 @@
         else:
             axis, by = STEPS[channel]
             axis = (axis + place[2]) % 2
-            to[axis] = (to[axis] + by * (1 - 2 * place[3] * MIRROR)) % DIMS[axis]
+            to[axis] = (to[axis] + by * (1 - 2 * place[3])) % DIMS[axis]
         pairs.append((row_of(place), row_of(to)))
     return pairs
 
@@ -80,8 +85,7 @@
     row = where[0]
     h = (row >> 1) & 1
     sign = 1 - 2 * ((row & 1) ^ core_flip)
-    if MIRROR:
-        a, b = a * sign, b * sign
+    a, b = a * sign, b * sign
     z = ((row >> 4) + a + h * (b - a)) & 3
     y = (((row >> 2) & 3) + b + h * (a - b)) & 3
     return (((z * 4 + y) * 2 + (h ^ t)) << 1) + ((row & 1) ^ core_flip)

time: 85.3 us -> 84.6 us (level); the launches traced: 85.4 us -> 83.4 us
  Pallas kernels: 27.3 us -> 23 us
  waiting for transfers between devices: 21.7 us -> 23.7 us
  other arithmetic: 1.9 us -> 2.8 us
    pallas_call x5, Pallas kernels: 17.7 us -> 13 us  [terms(): pl.pallas_call(functools.partial(terms_kernel, layout, half), out_shape=j...]
    ppermute x24, waiting for transfers between devices: 15.9 us -> 19.4 us  [send(): return lax.ppermute(x, 'row', pairs_of(channel))]
    ppermute x1, waiting for transfers between devices: 5.8 us -> 4.33 us  [body(): received = lax.ppermute(sent.astype(jnp.bfloat16), 'rep', [(0, 1), (1, 0)])]
    ppermute x24, starting transfers between devices: 32.9 us -> 31.7 us  [send(): return lax.ppermute(x, 'row', pairs_of(channel))]
    concatenate x2 -> x5, other arithmetic: 1.09 us -> 1.99 us  [payload(): return (x[0] if len(x) == 1 else jnp.concatenate(x), units)]
  transfers between devices with their start and end apart: 25 -> 25, of which waited for: 11 -> 11; matrix products, arithmetic and copies ran while one was open for 2% -> 4% of each run, Pallas kernels for 27% -> 22%
where the time goes in v1:
time: 84.6 us; the launch traced here: 83.4 us
  starting transfers between devices  32.3 us (38%)
  waiting for transfers between devices  23.7 us (28%)
  Pallas kernels  23 us (27%)
  other arithmetic  2.8 us (3%)
  matrix products  1.08 us (1%)
    ppermute x24, starting transfers between devices, send(): return lax.ppermute(x, 'row', pairs_of(channel))  31.7 us
    ppermute x24, waiting for transfers between devices, send(): return lax.ppermute(x, 'row', pairs_of(channel))  19.4 us
    pallas_call x5, Pallas kernels, terms(): pl.pallas_call(functools.partial(terms_kernel, layout, half), out_shape=j...  13 us
    pallas_call x1, Pallas kernels, load(): pl.pallas_call(load_kernel, out_shape=pltpu.VMEM(blocks.shape, blocks.dty...  5.82 us
    ppermute x1, waiting for transfers between devices, body(): received = lax.ppermute(sent.astype(jnp.bfloat16), 'rep', [(0, 1), (1, 0)])  4.33 us
    pallas_call x4, Pallas kernels, pack(): pl.pallas_call(functools.partial(pack_kernel, layout, 0 if into is None e...  4.17 us
    concatenate x5, other arithmetic, payload(): return (x[0] if len(x) == 1 else jnp.concatenate(x), units)  1.99 us
  transfers between devices with their start and end apart: 25, of which 11 were waited for; matrix products, arithmetic and copies ran while one was open for 4% of the time, Pallas kernels for 22%

profile of v1, /device:TPU:1, one launch (start us, length us, event | category | flops | bytes accessed | tf_op | source)
XLA Modules:
  0.0 83.4 jit_solution(4251322899713087024)
XLA Ops:
  0.0 2.5 %collective-permute-start.3 = (bf16[1024,128]{1,0:T(8,128)(2,1)}, bf16[1024,128]{1,0:T(8,128)(2,1)S(1)}, u32[]{:S(2)}, u32[]{:S(2)}) collective-permute-start(bf16[1024,128]{1,0:T(8,128)(2,1)} %refs_0_.3), channel_id=1, source_target_pairs={{0,48},{1,17},{2,14},{3,7},{4,52},{5,21},{6,2},{7,11},{8,56},{9,25... | collective-permute-start | bytes 786440 | tf_op jit(solution)/shard_map/ppermute | solution.py:80
  2.5 2.7 %collective-permute-start.2 = (bf16[1024,128]{1,0:T(8,128)(2,1)}, bf16[1024,128]{1,0:T(8,128)(2,1)S(1)}, u32[]{:S(2)}, u32[]{:S(2)}) collective-permute-start(bf16[1024,128]{1,0:T(8,128)(2,1)} %refs_0_.3), channel_id=1, source_target_pairs={{0,4},{1,13},{2,18},{3,51},{4,8},{5,1},{6,22},{7,55},{8,12},{9,5},... | collective-permute-start | bytes 786440 | tf_op jit(solution)/shard_map/ppermute | solution.py:80
  5.2 2.2 %collective-permute-start = (bf16[1024,128]{1,0:T(8,128)(2,1)}, bf16[1024,128]{1,0:T(8,128)(2,1)S(1)}, u32[]{:S(2)}, u32[]{:S(2)}) collective-permute-start(bf16[1024,128]{1,0:T(8,128)(2,1)} %refs_0_.3), channel_id=1, source_target_pairs={{0,16},{1,49},{2,6},{3,15},{4,20},{5,53},{6,10},{7,3},{8,24},{9,57... | collective-permute-start | bytes 786440 | tf_op jit(solution)/shard_map/ppermute | solution.py:80
  7.4 2.7 %collective-permute-start.1 = (bf16[1024,128]{1,0:T(8,128)(2,1)}, bf16[1024,128]{1,0:T(8,128)(2,1)S(1)}, u32[]{:S(2)}, u32[]{:S(2)}) collective-permute-start(bf16[1024,128]{1,0:T(8,128)(2,1)} %refs_0_.3), channel_id=1, source_target_pairs={{0,2},{1,3},{2,0},{3,1},{4,6},{5,7},{6,4},{7,5},{8,10},{9,11},{10,... | collective-permute-start | bytes 786440 | tf_op jit(solution)/shard_map/ppermute | solution.py:80
  10.9 1.5 %collective-permute-start.5 = (s32[3,64]{1,0:T(4,128)S(1)}, s32[3,64]{1,0:T(4,128)S(1)}, u32[]{:S(2)}, u32[]{:S(2)}) collective-permute-start(s32[3,64]{1,0:T(4,128)S(1)} %pad_add_fusion.codes), channel_id=1, source_target_pairs={{0,1},{1,0},{2,3},{3,2},{4,5},{5,4},{6,7},{7,6},{8,9},{9,8},{10,11... | collective-permute-start | bytes 2312 | tf_op jit(solution)/shard_map/ppermute | solution.py:80
  12.4 1.8 %collective-permute-done.4 = bf16[1024,128]{1,0:T(8,128)(2,1)S(1)} collective-permute-done((bf16[1024,128]{1,0:T(8,128)(2,1)}, bf16[1024,128]{1,0:T(8,128)(2,1)S(1)}, u32[]{:S(2)}, u32[]{:S(2)}) %collective-permute-start.4) | collective-permute-done | bytes 262176 | tf_op jit(solution)/shard_map/ppermute | solution.py:80
  14.2 1.1 %pad_maximum_fusion.3 = (bf16[2048,128]{1,0:T(8,128)(2,1)}, bf16[2048,128]{1,0:T(8,128)(2,1)}) fusion(bf16[1024,128]{1,0:T(8,128)(2,1)S(1)} %collective-permute-done.4, bf16[1024,128]{1,0:T(8,128)(2,1)S(1)} %collective-permute-done.3.refs_3_, bf16[1024,128]{1,0:T(8,128)(2,1)S(1)} %collective-permute-done.2), kind=kLoop, calls=%fused_computation.6 | loop fusion | flops 2097152 | bytes 1835008 | tf_op jit(solution)/shard_map/concatenate | solution.py:283
  15.5 4.0 %collective-permute-start.8 = (bf16[2048,128]{1,0:T(8,128)(2,1)}, bf16[2048,128]{1,0:T(8,128)(2,1)S(1)}, u32[]{:S(2)}, u32[]{:S(2)}) collective-permute-start(bf16[2048,128]{1,0:T(8,128)(2,1)} %get-tuple-element.37), channel_id=1, source_target_pairs={{0,2},{1,3},{2,0},{3,1},{4,6},{5,7},{6,4},{7,5},{8,10},{9,11},{10,... | collective-permute-start | bytes 1572872 | tf_op jit(solution)/shard_map/ppermute | solution.py:80
  19.8 2.7 %collective-permute-start.9 = (bf16[2048,128]{1,0:T(8,128)(2,1)S(1)}, bf16[2048,128]{1,0:T(8,128)(2,1)}, u32[]{:S(2)}, u32[]{:S(2)}) collective-permute-start(bf16[2048,128]{1,0:T(8,128)(2,1)S(1)} %constant_dynamic-update-slice_fusion.2.refs_2_), channel_id=1, source_target_pairs={{0,16},{1,49},{2,6},{3,15},{4,20},{5,53},{6,10},{7,3},{8,24},{9,57... | collective-permute-start | bytes 1572872 | tf_op jit(solution)/shard_map/ppermute | solution.py:80
  23.5 5.8 %load.1.blocks = bf16[64,2,256,256]{3,2,1,0:T(8,128)(2,1)S(1)} custom-call(bf16[64,2,256,256]{3,2,1,0:T(8,128)(2,1)} %bitcast.8), custom_call_target="tpu_custom_call" | custom-call | bytes 16777216 | tf_op jit(solution)/shard_map/load/pallas_call | solution.py:252
  30.3 3.0 %collective-permute-done.9.refs_3_.refs_7_ = bf16[2048,128]{1,0:T(8,128)(2,1)} collective-permute-done((bf16[2048,128]{1,0:T(8,128)(2,1)S(1)}, bf16[2048,128]{1,0:T(8,128)(2,1)}, u32[]{:S(2)}, u32[]{:S(2)}) %collective-permute-start.9) | collective-permute-done | bytes 524320 | tf_op jit(solution)/shard_map/ppermute | solution.py:80
  33.3 1.5 %pack.5 = bf16[32,256,128]{2,1,0:T(8,128)(2,1)S(1)} custom-call(s32[2]{0:T(128)S(1)} %pad_add_fusion.1.where, s32[3,64]{1,0:T(4,128)S(1)} %collective-permute-done.5.codes, bf16[2048,128]{1,0:T(8,128)(2,1)S(1)} %collective-permute-done.7.refs_0_.refs_4_, ...), custom_call_target="tpu_custom_call", output_to_operand_aliasing={{}: (7, {})} | custom-call | bytes 2621440 | tf_op jit(solution)/shard_map/pack/pallas_call | solution.py:117
  34.8 4.2 %collective-permute-start.11 = (bf16[32,256,128]{2,1,0:T(8,128)(2,1)S(1)}, bf16[32,256,128]{2,1,0:T(8,128)(2,1)S(1)}, u32[]{:S(2)}, u32[]{:S(2)}) collective-permute-start(bf16[32,256,128]{2,1,0:T(8,128)(2,1)S(1)} %pack.5), channel_id=1, source_target_pairs={{0,1},{1,0},{2,3},{3,2},{4,5},{5,4},{6,7},{7,6},{8,9},{9,8},{10,11... | collective-permute-start | bytes 6291464 | tf_op jit(solution)/shard_map/ppermute | solution.py:80
  40.2 2.6 %collective-permute-done.11.refs_9_ = bf16[32,256,128]{2,1,0:T(8,128)(2,1)S(1)} collective-permute-done((bf16[32,256,128]{2,1,0:T(8,128)(2,1)S(1)}, bf16[32,256,128]{2,1,0:T(8,128)(2,1)S(1)}, u32[]{:S(2)}, u32[]{:S(2)}) %collective-permute-start.11) | collective-permute-done | bytes 2097184 | tf_op jit(solution)/shard_map/ppermute | solution.py:80
  42.8 1.0 %collective-permute-start.16 = (bf16[2048,128]{1,0:T(8,128)(2,1)S(1)}, bf16[2048,128]{1,0:T(8,128)(2,1)S(1)}, u32[]{:S(2)}, u32[]{:S(2)}) collective-permute-start(bf16[2048,128]{1,0:T(8,128)(2,1)S(1)} %collective-permute-done.6.refs_2_.refs_6_), channel_id=1, source_target_pairs={{0,16},{1,49},{2,6},{3,15},{4,20},{5,53},{6,10},{7,3},{8,24},{9,57... | collective-permute-start | bytes 1572872 | tf_op jit(solution)/shard_map/ppermute | solution.py:80
  43.8 0.9 %collective-permute-start.12 = (bf16[2048,128]{1,0:T(8,128)(2,1)S(1)}, bf16[2048,128]{1,0:T(8,128)(2,1)S(1)}, u32[]{:S(2)}, u32[]{:S(2)}) collective-permute-start(bf16[2048,128]{1,0:T(8,128)(2,1)S(1)} %pad_maximum_fusion.1), channel_id=1, source_target_pairs={{0,4},{1,13},{2,18},{3,51},{4,8},{5,1},{6,22},{7,55},{8,12},{9,5},... | collective-permute-start | bytes 1572872 | tf_op jit(solution)/shard_map/ppermute | solution.py:80
  44.7 5.4 %terms.5.refs_6_ = f32[2048,128]{1,0:T(8,128)S(1)} custom-call(s32[2]{0:T(128)S(1)} %pad_add_fusion.1.where, s32[3,64]{1,0:T(4,128)S(1)} %pad_add_fusion.codes, bf16[64,2,256,256]{3,2,1,0:T(8,128)(2,1)S(1)} %load.1.blocks, bf16[1024,128]{1,0:T(8,128)(2,1)S(1)} %copy-done.1, bf16[2048,128]{1,0:T(8,128)(2,1)S(1)} %constant_dynamic-update-slice_fusion.refs_1_, ...), custom_call_target="tpu_custom_call" | custom-call | flops 1073741824 | bytes 12582912 | tf_op jit(solution)/shard_map/terms/pallas_call | solution.py:229
  50.1 3.0 %collective-permute-done.14.refs_1_ = bf16[2048,128]{1,0:T(8,128)(2,1)S(1)} collective-permute-done((bf16[2048,128]{1,0:T(8,128)(2,1)S(1)}, bf16[2048,128]{1,0:T(8,128)(2,1)S(1)}, u32[]{:S(2)}, u32[]{:S(2)}) %collective-permute-start.14) | collective-permute-done | bytes 524320 | tf_op jit(solution)/shard_map/ppermute | solution.py:80
  53.6 2.6 %collective-permute-done.12.refs_3_ = bf16[2048,128]{1,0:T(8,128)(2,1)S(1)} collective-permute-done((bf16[2048,128]{1,0:T(8,128)(2,1)S(1)}, bf16[2048,128]{1,0:T(8,128)(2,1)S(1)}, u32[]{:S(2)}, u32[]{:S(2)}) %collective-permute-start.12) | collective-permute-done | bytes 524320 | tf_op jit(solution)/shard_map/ppermute | solution.py:80
  56.2 1.0 %pack.6 = bf16[20,256,128]{2,1,0:T(8,128)(2,1)S(1)} custom-call(s32[2]{0:T(128)S(1)} %pad_add_fusion.1.where, s32[3,64]{1,0:T(4,128)S(1)} %collective-permute-done.5.codes, bf16[2048,128]{1,0:T(8,128)(2,1)S(1)} %collective-permute-done.13.refs_0_, bf16[2048,128]{1,0:T(8,128)(2,1)S(1)} %collective-permute-done.14.refs_1_, ...), custom_call_target="tpu_custom_call" | custom-call | bytes 2621440 | tf_op jit(solution)/shard_map/pack/pallas_call | solution.py:117
  57.7 1.4 %collective-permute-start.20 = (bf16[1024,128]{1,0:T(8,128)(2,1)S(1)}, bf16[1024,128]{1,0:T(8,128)(2,1)S(1)}, u32[]{:S(2)}, u32[]{:S(2)}) collective-permute-start(bf16[1024,128]{1,0:T(8,128)(2,1)S(1)} %get-tuple-element.58), channel_id=1, source_target_pairs={{0,32},{1,33},{2,10},{3,11},{4,36},{5,37},{6,14},{7,15},{8,40},{9,... | collective-permute-start | bytes 786440 | tf_op jit(solution)/shard_map/ppermute | solution.py:80
  59.1 1.8 %collective-permute-start.19 = (bf16[1024,128]{1,0:T(8,128)(2,1)S(1)}, bf16[1024,128]{1,0:T(8,128)(2,1)S(1)}, u32[]{:S(2)}, u32[]{:S(2)}) collective-permute-start(bf16[1024,128]{1,0:T(8,128)(2,1)S(1)} %slice.44), channel_id=1, source_target_pairs={{0,2},{1,3},{2,0},{3,1},{4,6},{5,7},{6,4},{7,5},{8,10},{9,11},{10,... | collective-permute-start | bytes 786440 | tf_op jit(solution)/shard_map/ppermute | solution.py:80
  61.5 1.2 %collective-permute-start.22 = (bf16[1024,128]{1,0:T(8,128)(2,1)S(1)}, bf16[1024,128]{1,0:T(8,128)(2,1)S(1)}, u32[]{:S(2)}, u32[]{:S(2)}) collective-permute-start(bf16[1024,128]{1,0:T(8,128)(2,1)S(1)} %slice.42), channel_id=1, source_target_pairs={{0,4},{1,13},{2,18},{3,51},{4,8},{5,1},{6,22},{7,55},{8,12},{9,5},... | collective-permute-start | bytes 786440 | tf_op jit(solution)/shard_map/ppermute | solution.py:80
  62.6 3.1 %terms.6.refs_6_.refs_5_ = f32[2048,128]{1,0:T(8,128)S(1)} custom-call(s32[2]{0:T(128)S(1)} %pad_add_fusion.1.where, s32[3,64]{1,0:T(4,128)S(1)} %pad_add_fusion.codes, bf16[64,2,256,256]{3,2,1,0:T(8,128)(2,1)S(1)} %load.1.blocks, bf16[2048,128]{1,0:T(8,128)(2,1)S(1)} %collective-permute-done.13.refs_0_, ...), custom_call_target="tpu_custom_call" | custom-call | flops 671088640 | bytes 7864320 | tf_op jit(solution)/shard_map/terms/pallas_call | solution.py:229
  65.7 0.8 %collective-permute-done.19.refs_2_ = bf16[1024,128]{1,0:T(8,128)(2,1)S(1)} collective-permute-done((bf16[1024,128]{1,0:T(8,128)(2,1)S(1)}, bf16[1024,128]{1,0:T(8,128)(2,1)S(1)}, u32[]{:S(2)}, u32[]{:S(2)}) %collective-permute-start.19) | collective-permute-done | bytes 262176 | tf_op jit(solution)/shard_map/ppermute | solution.py:80
  66.5 3.9 %collective-permute-done.17.refs_0_ = bf16[1024,128]{1,0:T(8,128)(2,1)S(1)} collective-permute-done((bf16[1024,128]{1,0:T(8,128)(2,1)S(1)}, bf16[1024,128]{1,0:T(8,128)(2,1)S(1)}, u32[]{:S(2)}, u32[]{:S(2)}) %collective-permute-start.17) | collective-permute-done | bytes 262176 | tf_op jit(solution)/shard_map/ppermute | solution.py:80
  72.0 1.1 %terms.8.refs_1_ = f32[1024,128]{1,0:T(8,128)S(1)} custom-call(s32[2]{0:T(128)S(1)} %pad_add_fusion.1.where, s32[3,64]{1,0:T(4,128)S(1)} %pad_add_fusion.codes, bf16[64,2,256,256]{3,2,1,0:T(8,128)(2,1)S(1)} %load.1.blocks, bf16[1024,128]{1,0:T(8,128)(2,1)S(1)} %collective-permute-done.17.refs_0_, bf16[2048,128]{1,0:T(8,128)(2,1)S(1)} %collective-permute-done.18.refs_1_, ...), custom_call_target="tpu_custom_call" | custom-call | flops 201326592 | bytes 2359296 | tf_op jit(solution)/shard_map/terms/pallas_call | solution.py:229
  73.0 0.9 %collective-permute-done.23.refs_5_.refs_0_ = bf16[12,256,128]{2,1,0:T(8,128)(2,1)S(1)} collective-permute-done((bf16[12,256,128]{2,1,0:T(8,128)(2,1)S(1)}, bf16[12,256,128]{2,1,0:T(8,128)(2,1)S(1)}, u32[]{:S(2)}, u32[]{:S(2)}) %collective-permute-start.23) | collective-permute-done | bytes 786464 | tf_op jit(solution)/shard_map/ppermute | solution.py:80
  73.9 1.4 %terms.9 = f32[1024,128]{1,0:T(8,128)S(1)} custom-call(s32[2]{0:T(128)S(1)} %pad_add_fusion.1.where, s32[3,64]{1,0:T(4,128)S(1)} %pad_add_fusion.codes, bf16[64,2,256,256]{3,2,1,0:T(8,128)(2,1)S(1)} %load.1.blocks, bf16[12,256,128]{2,1,0:T(8,128)(2,1)S(1)} %collective-permute-done.23.refs_5_.refs_0_, f32[1024,128]{1,0:T(8,128)S(1)} %terms.8.refs_1_), custom_call_target="tpu_custom_call" | custom-call | flops 201326592 | bytes 2359296 | tf_op jit(solution)/shard_map/terms/pallas_call | solution.py:229
  75.9 2.1 %terms.7 = f32[1024,128]{1,0:T(8,128)S(1)} custom-call(s32[2]{0:T(128)S(1)} %pad_add_fusion.1.where, s32[3,64]{1,0:T(4,128)S(1)} %pad_add_fusion.codes, bf16[64,2,256,256]{3,2,1,0:T(8,128)(2,1)S(1)} %load.1.blocks, bf16[1024,128]{1,0:T(8,128)(2,1)S(1)} %collective-permute-done.17.refs_0_, bf16[2048,128]{1,0:T(8,128)(2,1)S(1)} %collective-permute-done.18.refs_1_, ...), custom_call_target="tpu_custom_call" | custom-call | flops 402653184 | bytes 4718592 | tf_op jit(solution)/shard_map/terms/pallas_call | solution.py:229
  78.0 4.3 %collective-permute-done.24 = bf16[1024,128]{1,0:T(8,128)(2,1)S(1)} collective-permute-done((bf16[1024,128]{1,0:T(8,128)(2,1)S(1)}, bf16[1024,128]{1,0:T(8,128)(2,1)S(1)}, u32[]{:S(2)}, u32[]{:S(2)}) %collective-permute-start.24) | collective-permute-done | bytes 262176 | tf_op jit(solution)/shard_map/ppermute | solution.py:350
  82.3 1.1 %fusion.1 = bf16[1024,256]{1,0:T(8,128)(2,1)} fusion(bf16[128,256]{1,0:T(8,128)(2,1)S(1)} %copy-done, f32[256]{0:T(256)S(1)} %copy-done.2, f32[1024,128]{1,0:T(8,128)S(1)} %terms.7, bf16[1024,128]{1,0:T(8,128)(2,1)S(1)} %collective-permute-done.24), kind=kOutput, calls=%fused_computation.2 | convolution fusion | flops 68288512 | bytes 1377280 | tf_op jit(solution)/shard_map/dot_general | solution.py:352
  (54 shorter events, 8.0 us)
Async XLA Ops:
  0.0 82.3 %copy-start = (bf16[128,256]{1,0:T(8,128)(2,1)S(1)}, bf16[128,256]{1,0:T(8,128)(2,1)}, u32[]{:S(2)}) copy-start(bf16[128,256]{1,0:T(8,128)(2,1)} %param.10) | copy-start | bytes 196612
  0.0 10.8 %collective-permute-start.3 = (bf16[1024,128]{1,0:T(8,128)(2,1)}, bf16[1024,128]{1,0:T(8,128)(2,1)S(1)}, u32[]{:S(2)}, u32[]{:S(2)}) collective-permute-start(bf16[1024,128]{1,0:T(8,128)(2,1)} %refs_0_.3), channel_id=1, source_target_pairs={{0,48},{1,17},{2,14},{3,7},{4,52},{5,21},{6,2},{7,11},{8,56},{9,25... | collective-permute-start | bytes 786440 | tf_op jit(solution)/shard_map/ppermute | solution.py:80
  2.5 9.9 %collective-permute-start.2 = (bf16[1024,128]{1,0:T(8,128)(2,1)}, bf16[1024,128]{1,0:T(8,128)(2,1)S(1)}, u32[]{:S(2)}, u32[]{:S(2)}) collective-permute-start(bf16[1024,128]{1,0:T(8,128)(2,1)} %refs_0_.3), channel_id=1, source_target_pairs={{0,4},{1,13},{2,18},{3,51},{4,8},{5,1},{6,22},{7,55},{8,12},{9,5},... | collective-permute-start | bytes 786440 | tf_op jit(solution)/shard_map/ppermute | solution.py:80
  5.2 9.0 %collective-permute-start.4 = (bf16[1024,128]{1,0:T(8,128)(2,1)}, bf16[1024,128]{1,0:T(8,128)(2,1)S(1)}, u32[]{:S(2)}, u32[]{:S(2)}) collective-permute-start(bf16[1024,128]{1,0:T(8,128)(2,1)} %refs_0_.3), channel_id=1, source_target_pairs={{0,12},{1,5},{2,50},{3,19},{4,0},{5,9},{6,54},{7,23},{8,4},{9,13},... | collective-permute-start | bytes 786440 | tf_op jit(solution)/shard_map/ppermute | solution.py:80
  5.2 10.0 %collective-permute-start = (bf16[1024,128]{1,0:T(8,128)(2,1)}, bf16[1024,128]{1,0:T(8,128)(2,1)S(1)}, u32[]{:S(2)}, u32[]{:S(2)}) collective-permute-start(bf16[1024,128]{1,0:T(8,128)(2,1)} %refs_0_.3), channel_id=1, source_target_pairs={{0,16},{1,49},{2,6},{3,15},{4,20},{5,53},{6,10},{7,3},{8,24},{9,57... | collective-permute-start | bytes 786440 | tf_op jit(solution)/shard_map/ppermute | solution.py:80
  7.4 8.1 %collective-permute-start.1 = (bf16[1024,128]{1,0:T(8,128)(2,1)}, bf16[1024,128]{1,0:T(8,128)(2,1)S(1)}, u32[]{:S(2)}, u32[]{:S(2)}) collective-permute-start(bf16[1024,128]{1,0:T(8,128)(2,1)} %refs_0_.3), channel_id=1, source_target_pairs={{0,2},{1,3},{2,0},{3,1},{4,6},{5,7},{6,4},{7,5},{8,10},{9,11},{10,... | collective-permute-start | bytes 786440 | tf_op jit(solution)/shard_map/ppermute | solution.py:80
  10.9 4.4 %collective-permute-start.5 = (s32[3,64]{1,0:T(4,128)S(1)}, s32[3,64]{1,0:T(4,128)S(1)}, u32[]{:S(2)}, u32[]{:S(2)}) collective-permute-start(s32[3,64]{1,0:T(4,128)S(1)} %pad_add_fusion.codes), channel_id=1, source_target_pairs={{0,1},{1,0},{2,3},{3,2},{4,5},{5,4},{6,7},{7,6},{8,9},{9,8},{10,11... | collective-permute-start | bytes 2312 | tf_op jit(solution)/shard_map/ppermute | solution.py:80
  15.5 14.8 %collective-permute-start.10 = (bf16[2048,128]{1,0:T(8,128)(2,1)}, bf16[2048,128]{1,0:T(8,128)(2,1)S(1)}, u32[]{:S(2)}, u32[]{:S(2)}) collective-permute-start(bf16[2048,128]{1,0:T(8,128)(2,1)} %get-tuple-element.39), channel_id=1, source_target_pairs={{0,12},{1,5},{2,50},{3,19},{4,0},{5,9},{6,54},{7,23},{8,4},{9,13},... | collective-permute-start | bytes 1572872 | tf_op jit(solution)/shard_map/ppermute | solution.py:80
  15.5 14.8 %collective-permute-start.8 = (bf16[2048,128]{1,0:T(8,128)(2,1)}, bf16[2048,128]{1,0:T(8,128)(2,1)S(1)}, u32[]{:S(2)}, u32[]{:S(2)}) collective-permute-start(bf16[2048,128]{1,0:T(8,128)(2,1)} %get-tuple-element.37), channel_id=1, source_target_pairs={{0,2},{1,3},{2,0},{3,1},{4,6},{5,7},{6,4},{7,5},{8,10},{9,11},{10,... | collective-permute-start | bytes 1572872 | tf_op jit(solution)/shard_map/ppermute | solution.py:80
  19.6 10.7 %collective-permute-start.7 = (bf16[2048,128]{1,0:T(8,128)(2,1)S(1)}, bf16[2048,128]{1,0:T(8,128)(2,1)S(1)}, u32[]{:S(2)}, u32[]{:S(2)}) collective-permute-start(bf16[2048,128]{1,0:T(8,128)(2,1)S(1)} %constant_dynamic-update-slice_fusion.refs_1_), channel_id=1, source_target_pairs={{0,48},{1,17},{2,14},{3,7},{4,52},{5,21},{6,2},{7,11},{8,56},{9,25... | collective-permute-start | bytes 1572872 | tf_op jit(solution)/shard_map/ppermute | solution.py:80
  19.8 13.6 %collective-permute-start.9 = (bf16[2048,128]{1,0:T(8,128)(2,1)S(1)}, bf16[2048,128]{1,0:T(8,128)(2,1)}, u32[]{:S(2)}, u32[]{:S(2)}) collective-permute-start(bf16[2048,128]{1,0:T(8,128)(2,1)S(1)} %constant_dynamic-update-slice_fusion.2.refs_2_), channel_id=1, source_target_pairs={{0,16},{1,49},{2,6},{3,15},{4,20},{5,53},{6,10},{7,3},{8,24},{9,57... | collective-permute-start | bytes 1572872 | tf_op jit(solution)/shard_map/ppermute | solution.py:80
  23.3 10.0 %collective-permute-start.6 = (bf16[2048,128]{1,0:T(8,128)(2,1)}, bf16[2048,128]{1,0:T(8,128)(2,1)S(1)}, u32[]{:S(2)}, u32[]{:S(2)}) collective-permute-start(bf16[2048,128]{1,0:T(8,128)(2,1)} %pad_maximum_fusion), channel_id=1, source_target_pairs={{0,4},{1,13},{2,18},{3,51},{4,8},{5,1},{6,22},{7,55},{8,12},{9,5},... | collective-permute-start | bytes 1572872 | tf_op jit(solution)/shard_map/ppermute | solution.py:80
  23.5 5.9 %copy-start.1 = (bf16[1024,128]{1,0:T(8,128)(2,1)S(1)}, bf16[1024,128]{1,0:T(8,128)(2,1)}, u32[]{:S(2)}) copy-start(bf16[1024,128]{1,0:T(8,128)(2,1)} %refs_0_.3) | copy-start | bytes 786436
  34.8 8.0 %collective-permute-start.11 = (bf16[32,256,128]{2,1,0:T(8,128)(2,1)S(1)}, bf16[32,256,128]{2,1,0:T(8,128)(2,1)S(1)}, u32[]{:S(2)}, u32[]{:S(2)}) collective-permute-start(bf16[32,256,128]{2,1,0:T(8,128)(2,1)S(1)} %pack.5), channel_id=1, source_target_pairs={{0,1},{1,0},{2,3},{3,2},{4,5},{5,4},{6,7},{7,6},{8,9},{9,8},{10,11... | collective-permute-start | bytes 6291464 | tf_op jit(solution)/shard_map/ppermute | solution.py:80
  39.1 10.9 %collective-permute-start.15 = (bf16[2048,128]{1,0:T(8,128)(2,1)S(1)}, bf16[2048,128]{1,0:T(8,128)(2,1)S(1)}, u32[]{:S(2)}, u32[]{:S(2)}) collective-permute-start(bf16[2048,128]{1,0:T(8,128)(2,1)S(1)} %pad_maximum_fusion.4), channel_id=1, source_target_pairs={{0,48},{1,17},{2,14},{3,7},{4,52},{5,21},{6,2},{7,11},{8,56},{9,25... | collective-permute-start | bytes 1572872 | tf_op jit(solution)/shard_map/ppermute | solution.py:80
  39.2 13.8 %collective-permute-start.14 = (bf16[2048,128]{1,0:T(8,128)(2,1)S(1)}, bf16[2048,128]{1,0:T(8,128)(2,1)S(1)}, u32[]{:S(2)}, u32[]{:S(2)}) collective-permute-start(bf16[2048,128]{1,0:T(8,128)(2,1)S(1)} %collective-permute-done.10.refs_4_.refs_8_), channel_id=1, source_target_pairs={{0,2},{1,3},{2,0},{3,1},{4,6},{5,7},{6,4},{7,5},{8,10},{9,11},{10,... | collective-permute-start | bytes 1572872 | tf_op jit(solution)/shard_map/ppermute | solution.py:80
  39.5 13.5 %collective-permute-start.13 = (bf16[2048,128]{1,0:T(8,128)(2,1)S(1)}, bf16[2048,128]{1,0:T(8,128)(2,1)S(1)}, u32[]{:S(2)}, u32[]{:S(2)}) collective-permute-start(bf16[2048,128]{1,0:T(8,128)(2,1)S(1)} %collective-permute-done.8.refs_1_.refs_5_), channel_id=1, source_target_pairs={{0,12},{1,5},{2,50},{3,19},{4,0},{5,9},{6,54},{7,23},{8,4},{9,13},... | collective-permute-start | bytes 1572872 | tf_op jit(solution)/shard_map/ppermute | solution.py:80
  42.8 10.8 %collective-permute-start.16 = (bf16[2048,128]{1,0:T(8,128)(2,1)S(1)}, bf16[2048,128]{1,0:T(8,128)(2,1)S(1)}, u32[]{:S(2)}, u32[]{:S(2)}) collective-permute-start(bf16[2048,128]{1,0:T(8,128)(2,1)S(1)} %collective-permute-done.6.refs_2_.refs_6_), channel_id=1, source_target_pairs={{0,16},{1,49},{2,6},{3,15},{4,20},{5,53},{6,10},{7,3},{8,24},{9,57... | collective-permute-start | bytes 1572872 | tf_op jit(solution)/shard_map/ppermute | solution.py:80
  43.8 12.4 %collective-permute-start.12 = (bf16[2048,128]{1,0:T(8,128)(2,1)S(1)}, bf16[2048,128]{1,0:T(8,128)(2,1)S(1)}, u32[]{:S(2)}, u32[]{:S(2)}) collective-permute-start(bf16[2048,128]{1,0:T(8,128)(2,1)S(1)} %pad_maximum_fusion.1), channel_id=1, source_target_pairs={{0,4},{1,13},{2,18},{3,51},{4,8},{5,1},{6,22},{7,55},{8,12},{9,5},... | collective-permute-start | bytes 1572872 | tf_op jit(solution)/shard_map/ppermute | solution.py:80
  57.2 4.2 %collective-permute-start.21 = (bf16[20,256,128]{2,1,0:T(8,128)(2,1)S(1)}, bf16[20,256,128]{2,1,0:T(8,128)(2,1)S(1)}, u32[]{:S(2)}, u32[]{:S(2)}) collective-permute-start(bf16[20,256,128]{2,1,0:T(8,128)(2,1)S(1)} %pack.6), channel_id=1, source_target_pairs={{0,1},{1,0},{2,3},{3,2},{4,5},{5,4},{6,7},{7,6},{8,9},{9,8},{10,11... | collective-permute-start | bytes 3932168 | tf_op jit(solution)/shard_map/ppermute | solution.py:80
  57.4 13.0 %collective-permute-start.18 = (bf16[2048,128]{1,0:T(8,128)(2,1)S(1)}, bf16[2048,128]{1,0:T(8,128)(2,1)S(1)}, u32[]{:S(2)}, u32[]{:S(2)}) collective-permute-start(bf16[2048,128]{1,0:T(8,128)(2,1)S(1)} %pad_maximum_fusion.5), channel_id=1, source_target_pairs={{0,12},{1,5},{2,50},{3,19},{4,0},{5,9},{6,54},{7,23},{8,4},{9,13},... | collective-permute-start | bytes 1572872 | tf_op jit(solution)/shard_map/ppermute | solution.py:80
  57.7 8.0 %collective-permute-start.20 = (bf16[1024,128]{1,0:T(8,128)(2,1)S(1)}, bf16[1024,128]{1,0:T(8,128)(2,1)S(1)}, u32[]{:S(2)}, u32[]{:S(2)}) collective-permute-start(bf16[1024,128]{1,0:T(8,128)(2,1)S(1)} %get-tuple-element.58), channel_id=1, source_target_pairs={{0,32},{1,33},{2,10},{3,11},{4,36},{5,37},{6,14},{7,15},{8,40},{9,... | collective-permute-start | bytes 786440 | tf_op jit(solution)/shard_map/ppermute | solution.py:80
  59.1 7.4 %collective-permute-start.19 = (bf16[1024,128]{1,0:T(8,128)(2,1)S(1)}, bf16[1024,128]{1,0:T(8,128)(2,1)S(1)}, u32[]{:S(2)}, u32[]{:S(2)}) collective-permute-start(bf16[1024,128]{1,0:T(8,128)(2,1)S(1)} %slice.44), channel_id=1, source_target_pairs={{0,2},{1,3},{2,0},{3,1},{4,6},{5,7},{6,4},{7,5},{8,10},{9,11},{10,... | collective-permute-start | bytes 786440 | tf_op jit(solution)/shard_map/ppermute | solution.py:80
  61.0 9.5 %collective-permute-start.17 = (bf16[1024,128]{1,0:T(8,128)(2,1)S(1)}, bf16[1024,128]{1,0:T(8,128)(2,1)S(1)}, u32[]{:S(2)}, u32[]{:S(2)}) collective-permute-start(bf16[1024,128]{1,0:T(8,128)(2,1)S(1)} %slice.39), channel_id=1, source_target_pairs={{0,48},{1,17},{2,14},{3,7},{4,52},{5,21},{6,2},{7,11},{8,56},{9,25... | collective-permute-start | bytes 786440 | tf_op jit(solution)/shard_map/ppermute | solution.py:80
  61.5 9.0 %collective-permute-start.22 = (bf16[1024,128]{1,0:T(8,128)(2,1)S(1)}, bf16[1024,128]{1,0:T(8,128)(2,1)S(1)}, u32[]{:S(2)}, u32[]{:S(2)}) collective-permute-start(bf16[1024,128]{1,0:T(8,128)(2,1)S(1)} %slice.42), channel_id=1, source_target_pairs={{0,4},{1,13},{2,18},{3,51},{4,8},{5,1},{6,22},{7,55},{8,12},{9,5},... | collective-permute-start | bytes 786440 | tf_op jit(solution)/shard_map/ppermute | solution.py:80
  71.3 2.6 %collective-permute-start.23 = (bf16[12,256,128]{2,1,0:T(8,128)(2,1)S(1)}, bf16[12,256,128]{2,1,0:T(8,128)(2,1)S(1)}, u32[]{:S(2)}, u32[]{:S(2)}) collective-permute-start(bf16[12,256,128]{2,1,0:T(8,128)(2,1)S(1)} %pack.7), channel_id=1, source_target_pairs={{0,1},{1,0},{2,3},{3,2},{4,5},{5,4},{6,7},{7,6},{8,9},{9,8},{10,11... | collective-permute-start | bytes 2359304 | tf_op jit(solution)/shard_map/ppermute | solution.py:80
  75.3 7.0 %copy-start.2 = (f32[256]{0:T(256)S(1)}, f32[256]{0:T(256)}, u32[]{:S(2)}) copy-start(f32[256]{0:T(256)} %param.11) | copy-start | bytes 3076
  75.3 7.0 %collective-permute-start.24 = (bf16[1024,128]{1,0:T(8,128)(2,1)S(1)}, bf16[1024,128]{1,0:T(8,128)(2,1)S(1)}, u32[]{:S(2)}, u32[]{:S(2)}) collective-permute-start(bf16[1024,128]{1,0:T(8,128)(2,1)S(1)} %convert_element_type.12), channel_id=1, source_target_pairs={{0,64},{64,0},{1,65},{65,1},{2,66},{66,2},{3,67},{67,3},{4,68},{68... | collective-permute-start | bytes 786440 | tf_op jit(solution)/shard_map/ppermute | solution.py:350

commit v2 on v1

--- a/solution.py
+++ b/solution.py
@@ -15,18 +15,18 @@
 HOME = (0, 0, 0)
 ROUNDS = (
     (
+        ("M1", (HOME,)),
+        ("M2", (HOME,)),
+        ("X", (HOME,)),
         ("P2", (HOME,)),
-        ("M1", (HOME,)),
         ("P1", (HOME,)),
-        ("X", (HOME,)),
-        ("M2", (HOME,)),
     ),
     (
-        ("M1", ((1, 0, 0), (0, 0, 3))),
-        ("X", ((0, 0, 3), (0, 1, 0))),
-        ("P2", ((0, 3, 0), (1, 0, 0))),
         ("P1", ((0, 0, 1), (0, 3, 0))),
         ("M2", ((0, 1, 0), (0, 0, 1))),
+        ("X", ((0, 0, 3), (0, 1, 0))),
+        ("M1", ((1, 0, 0), (0, 0, 3))),
+        ("P2", ((0, 3, 0), (1, 0, 0))),
     ),
     (
         ("M2", ((1, 3, 0), (1, 0, 1))),
@@ -36,14 +36,14 @@
         ("P1", ((0, 3, 3), (1, 0, 3))),
     ),
     (
+        ("M2", ((1, 2, 0), (1, 3, 1))),
+        ("P2", ((1, 2, 0),)),
+        ("D1", ((1, 0, 2),)),
+        ("X", ((0, 2, 1),)),
         ("M1", ((0, 1, 2),)),
-        ("M2", ((1, 2, 0), (1, 3, 1))),
-        ("X", ((0, 2, 1),)),
-        ("D1", ((1, 0, 2),)),
-        ("P2", ((1, 2, 0),)),
     ),
 )
-LATE = ((), (), ("P1", "P2"), ("P2",))
+LATE = ((), (), ("P1", "M2"), ("P2",))
 WIDTH = (2, 4)
 STEPS = {"P1": (0, 1), "M1": (0, -1), "D1": (0, 2), "D2": (1, 2), "P2": (1, 1), "M2": (1, -1)}
 

time: 84.6 us -> 82.9 us (0.980)
  waiting for transfers between devices: 23.7 us -> 21.5 us
  starting transfers between devices: 32.3 us -> 34 us
  Pallas kernels: 23 us -> 21.7 us
    ppermute x24, waiting for transfers between devices: 19.4 us -> 17.7 us  [send(): return lax.ppermute(x, 'row', pairs_of(channel))]
    pallas_call x5, Pallas kernels: 13 us -> 11.8 us  [terms(): pl.pallas_call(functools.partial(terms_kernel, layout, half), out_shape=j...]
    ppermute x24, starting transfers between devices: 31.7 us -> 32.7 us  [send(): return lax.ppermute(x, 'row', pairs_of(channel))]
  transfers between devices with their start and end apart: 25 -> 25, of which waited for: 11 -> 12; matrix products, arithmetic and copies ran while one was open for 4% -> 4% of each run, Pallas kernels for 22% -> 21%
where the time goes in v2:
time: 82.9 us; the launch traced here: 81.6 us
  starting transfers between devices  34 us (41%)
  Pallas kernels  21.7 us (26%)
  waiting for transfers between devices  21.5 us (26%)
  other arithmetic  2.79 us (3%)
  matrix products  1.08 us (1%)
    ppermute x24, starting transfers between devices, send(): return lax.ppermute(x, 'row', pairs_of(channel))  32.7 us
    ppermute x24, waiting for transfers between devices, send(): return lax.ppermute(x, 'row', pairs_of(channel))  17.7 us
    pallas_call x5, Pallas kernels, terms(): pl.pallas_call(functools.partial(terms_kernel, layout, half), out_shape=j...  11.8 us
    pallas_call x1, Pallas kernels, load(): pl.pallas_call(load_kernel, out_shape=pltpu.VMEM(blocks.shape, blocks.dty...  5.82 us
    pallas_call x4, Pallas kernels, pack(): pl.pallas_call(functools.partial(pack_kernel, layout, 0 if into is None e...  4.16 us
    ppermute x1, waiting for transfers between devices, body(): received = lax.ppermute(sent.astype(jnp.bfloat16), 'rep', [(0, 1), (1, 0)])  3.79 us
    concatenate x5, other arithmetic, payload(): return (x[0] if len(x) == 1 else jnp.concatenate(x), units)  1.98 us
  transfers between devices with their start and end apart: 25, of which 12 were waited for; matrix products, arithmetic and copies ran while one was open for 4% of the time, Pallas kernels for 21%

profile of v2, /device:TPU:1, one launch (start us, length us, event | category | flops | bytes accessed | tf_op | source)
XLA Modules:
  0.0 81.6 jit_solution(6493401123102795581)
XLA Ops:
  0.0 3.6 %collective-permute-start.2 = (bf16[1024,128]{1,0:T(8,128)(2,1)}, bf16[1024,128]{1,0:T(8,128)(2,1)S(1)}, u32[]{:S(2)}, u32[]{:S(2)}) collective-permute-start(bf16[1024,128]{1,0:T(8,128)(2,1)} %refs_0_.3), channel_id=1, source_target_pairs={{0,2},{1,3},{2,0},{3,1},{4,6},{5,7},{6,4},{7,5},{8,10},{9,11},{10,... | collective-permute-start | bytes 786440 | tf_op jit(solution)/shard_map/ppermute | solution.py:80
  3.6 2.7 %collective-permute-start.3 = (bf16[1024,128]{1,0:T(8,128)(2,1)}, bf16[1024,128]{1,0:T(8,128)(2,1)S(1)}, u32[]{:S(2)}, u32[]{:S(2)}) collective-permute-start(bf16[1024,128]{1,0:T(8,128)(2,1)} %refs_0_.3), channel_id=1, source_target_pairs={{0,4},{1,13},{2,18},{3,51},{4,8},{5,1},{6,22},{7,55},{8,12},{9,5},... | collective-permute-start | bytes 786440 | tf_op jit(solution)/shard_map/ppermute | solution.py:80
  6.3 3.8 %collective-permute-start.4 = (bf16[1024,128]{1,0:T(8,128)(2,1)}, bf16[1024,128]{1,0:T(8,128)(2,1)S(1)}, u32[]{:S(2)}, u32[]{:S(2)}) collective-permute-start(bf16[1024,128]{1,0:T(8,128)(2,1)} %refs_0_.3), channel_id=1, source_target_pairs={{0,16},{1,49},{2,6},{3,15},{4,20},{5,53},{6,10},{7,3},{8,24},{9,57... | collective-permute-start | bytes 786440 | tf_op jit(solution)/shard_map/ppermute | solution.py:80
  10.8 1.8 %collective-permute-start.5 = (s32[3,64]{1,0:T(4,128)S(1)}, s32[3,64]{1,0:T(4,128)S(1)}, u32[]{:S(2)}, u32[]{:S(2)}) collective-permute-start(s32[3,64]{1,0:T(4,128)S(1)} %pad_add_fusion.codes), channel_id=1, source_target_pairs={{0,1},{1,0},{2,3},{3,2},{4,5},{5,4},{6,7},{7,6},{8,9},{9,8},{10,11... | collective-permute-start | bytes 2312 | tf_op jit(solution)/shard_map/ppermute | solution.py:80
  12.6 3.6 %collective-permute-done.4 = bf16[1024,128]{1,0:T(8,128)(2,1)S(1)} collective-permute-done((bf16[1024,128]{1,0:T(8,128)(2,1)}, bf16[1024,128]{1,0:T(8,128)(2,1)S(1)}, u32[]{:S(2)}, u32[]{:S(2)}) %collective-permute-start.4) | collective-permute-done | bytes 262176 | tf_op jit(solution)/shard_map/ppermute | solution.py:80
  16.2 1.0 %pad_maximum_fusion.2 = (bf16[2048,128]{1,0:T(8,128)(2,1)}, bf16[2048,128]{1,0:T(8,128)(2,1)}) fusion(bf16[1024,128]{1,0:T(8,128)(2,1)S(1)} %collective-permute-done.2.refs_3_, bf16[1024,128]{1,0:T(8,128)(2,1)S(1)} %collective-permute-done.4, bf16[1024,128]{1,0:T(8,128)(2,1)S(1)} %collective-permute-done.3), kind=kLoop, calls=%fused_computation.5 | loop fusion | flops 2097152 | bytes 1835008 | tf_op jit(solution)/shard_map/concatenate | solution.py:283
  17.3 1.2 %collective-permute-start.10 = (bf16[2048,128]{1,0:T(8,128)(2,1)}, bf16[2048,128]{1,0:T(8,128)(2,1)S(1)}, u32[]{:S(2)}, u32[]{:S(2)}) collective-permute-start(bf16[2048,128]{1,0:T(8,128)(2,1)} %get-tuple-element.39), channel_id=1, source_target_pairs={{0,4},{1,13},{2,18},{3,51},{4,8},{5,1},{6,22},{7,55},{8,12},{9,5},... | collective-permute-start | bytes 1572872 | tf_op jit(solution)/shard_map/ppermute | solution.py:80
  18.6 1.7 %collective-permute-start.8 = (bf16[2048,128]{1,0:T(8,128)(2,1)S(1)}, bf16[2048,128]{1,0:T(8,128)(2,1)S(1)}, u32[]{:S(2)}, u32[]{:S(2)}) collective-permute-start(bf16[2048,128]{1,0:T(8,128)(2,1)S(1)} %constant_dynamic-update-slice_fusion.2.refs_2_), channel_id=1, source_target_pairs={{0,2},{1,3},{2,0},{3,1},{4,6},{5,7},{6,4},{7,5},{8,10},{9,11},{10,... | collective-permute-start | bytes 1572872 | tf_op jit(solution)/shard_map/ppermute | solution.py:80
  20.4 1.1 %collective-permute-start.7 = (bf16[2048,128]{1,0:T(8,128)(2,1)S(1)}, bf16[2048,128]{1,0:T(8,128)(2,1)}, u32[]{:S(2)}, u32[]{:S(2)}) collective-permute-start(bf16[2048,128]{1,0:T(8,128)(2,1)S(1)} %constant_dynamic-update-slice_fusion.refs_1_), channel_id=1, source_target_pairs={{0,16},{1,49},{2,6},{3,15},{4,20},{5,53},{6,10},{7,3},{8,24},{9,57... | collective-permute-start | bytes 1572872 | tf_op jit(solution)/shard_map/ppermute | solution.py:80
  23.3 5.8 %load.1.blocks = bf16[64,2,256,256]{3,2,1,0:T(8,128)(2,1)S(1)} custom-call(bf16[64,2,256,256]{3,2,1,0:T(8,128)(2,1)} %bitcast.8), custom_call_target="tpu_custom_call" | custom-call | bytes 16777216 | tf_op jit(solution)/shard_map/load/pallas_call | solution.py:252
  30.0 1.3 %collective-permute-done.9.refs_3_.refs_7_ = bf16[2048,128]{1,0:T(8,128)(2,1)S(1)} collective-permute-done((bf16[2048,128]{1,0:T(8,128)(2,1)}, bf16[2048,128]{1,0:T(8,128)(2,1)S(1)}, u32[]{:S(2)}, u32[]{:S(2)}) %collective-permute-start.9) | collective-permute-done | bytes 524320 | tf_op jit(solution)/shard_map/ppermute | solution.py:80
  31.5 2.5 %collective-permute-done.7.refs_0_.refs_4_ = bf16[2048,128]{1,0:T(8,128)(2,1)} collective-permute-done((bf16[2048,128]{1,0:T(8,128)(2,1)S(1)}, bf16[2048,128]{1,0:T(8,128)(2,1)}, u32[]{:S(2)}, u32[]{:S(2)}) %collective-permute-start.7) | collective-permute-done | bytes 524320 | tf_op jit(solution)/shard_map/ppermute | solution.py:80
  34.1 1.5 %pack.5 = bf16[32,256,128]{2,1,0:T(8,128)(2,1)S(1)} custom-call(s32[2]{0:T(128)S(1)} %pad_add_fusion.1.where, s32[3,64]{1,0:T(4,128)S(1)} %collective-permute-done.5.codes, bf16[2048,128]{1,0:T(8,128)(2,1)} %collective-permute-done.7.refs_0_.refs_4_, bf16[2048,128]{1,0:T(8,128)(2,1)S(1)} %collective-permute-done.6.refs_1_.refs_5_, ...), custom_call_target="tpu_custom_call", output_to_operand_aliasing={{}: (7, {})} | custom-call | bytes 2621440 | tf_op jit(solution)/shard_map/pack/pallas_call | solution.py:117
  37.8 1.9 %collective-permute-start.11 = (bf16[2048,128]{1,0:T(8,128)(2,1)S(1)}, bf16[2048,128]{1,0:T(8,128)(2,1)S(1)}, u32[]{:S(2)}, u32[]{:S(2)}) collective-permute-start(bf16[2048,128]{1,0:T(8,128)(2,1)S(1)} %collective-permute-done.6.refs_1_.refs_5_), channel_id=1, source_target_pairs={{0,2},{1,3},{2,0},{3,1},{4,6},{5,7},{6,4},{7,5},{8,10},{9,11},{10,... | collective-permute-start | bytes 1572872 | tf_op jit(solution)/shard_map/ppermute | solution.py:80
  40.1 2.1 %collective-permute-start.16 = (bf16[2048,128]{1,0:T(8,128)(2,1)S(1)}, bf16[2048,128]{1,0:T(8,128)(2,1)S(1)}, u32[]{:S(2)}, u32[]{:S(2)}) collective-permute-start(bf16[2048,128]{1,0:T(8,128)(2,1)S(1)} %collective-permute-done.10.refs_4_.refs_8_), channel_id=1, source_target_pairs={{0,16},{1,49},{2,6},{3,15},{4,20},{5,53},{6,10},{7,3},{8,24},{9,57... | collective-permute-start | bytes 1572872 | tf_op jit(solution)/shard_map/ppermute | solution.py:80
  42.2 1.2 %collective-permute-start.13 = (bf16[2048,128]{1,0:T(8,128)(2,1)S(1)}, bf16[2048,128]{1,0:T(8,128)(2,1)S(1)}, u32[]{:S(2)}, u32[]{:S(2)}) collective-permute-start(bf16[2048,128]{1,0:T(8,128)(2,1)S(1)} %collective-permute-done.8.refs_2_.refs_6_), channel_id=1, source_target_pairs={{0,12},{1,5},{2,50},{3,19},{4,0},{5,9},{6,54},{7,23},{8,4},{9,13},... | collective-permute-start | bytes 1572872 | tf_op jit(solution)/shard_map/ppermute | solution.py:80
  43.5 4.5 %terms.5.refs_6_ = f32[2048,128]{1,0:T(8,128)S(1)} custom-call(s32[2]{0:T(128)S(1)} %pad_add_fusion.1.where, s32[3,64]{1,0:T(4,128)S(1)} %pad_add_fusion.codes, bf16[64,2,256,256]{3,2,1,0:T(8,128)(2,1)S(1)} %load.1.blocks, bf16[1024,128]{1,0:T(8,128)(2,1)S(1)} %copy-done.1, bf16[2048,128]{1,0:T(8,128)(2,1)S(1)} %constant_dynamic-update-slice_fusion.refs_1_, ...), custom_call_target="tpu_custom_call" | custom-call | flops 1073741824 | bytes 12582912 | tf_op jit(solution)/shard_map/terms/pallas_call | solution.py:229
  48.0 1.9 %collective-permute-done.11.refs_1_ = bf16[2048,128]{1,0:T(8,128)(2,1)S(1)} collective-permute-done((bf16[2048,128]{1,0:T(8,128)(2,1)S(1)}, bf16[2048,128]{1,0:T(8,128)(2,1)S(1)}, u32[]{:S(2)}, u32[]{:S(2)}) %collective-permute-start.11) | collective-permute-done | bytes 524320 | tf_op jit(solution)/shard_map/ppermute | solution.py:80
  50.9 3.5 %collective-permute-done.13.refs_3_ = bf16[2048,128]{1,0:T(8,128)(2,1)S(1)} collective-permute-done((bf16[2048,128]{1,0:T(8,128)(2,1)S(1)}, bf16[2048,128]{1,0:T(8,128)(2,1)S(1)}, u32[]{:S(2)}, u32[]{:S(2)}) %collective-permute-start.13) | collective-permute-done | bytes 524320 | tf_op jit(solution)/shard_map/ppermute | solution.py:80
  54.4 1.0 %pack.6 = bf16[20,256,128]{2,1,0:T(8,128)(2,1)S(1)} custom-call(s32[2]{0:T(128)S(1)} %pad_add_fusion.1.where, s32[3,64]{1,0:T(4,128)S(1)} %collective-permute-done.5.codes, bf16[2048,128]{1,0:T(8,128)(2,1)S(1)} %collective-permute-done.14.refs_0_, bf16[2048,128]{1,0:T(8,128)(2,1)S(1)} %collective-permute-done.11.refs_1_, ...), custom_call_target="tpu_custom_call" | custom-call | bytes 2621440 | tf_op jit(solution)/shard_map/pack/pallas_call | solution.py:117
  56.2 1.0 %collective-permute-start.20 = (bf16[1024,128]{1,0:T(8,128)(2,1)S(1)}, bf16[1024,128]{1,0:T(8,128)(2,1)S(1)}, u32[]{:S(2)}, u32[]{:S(2)}) collective-permute-start(bf16[1024,128]{1,0:T(8,128)(2,1)S(1)} %slice.45), channel_id=1, source_target_pairs={{0,48},{1,17},{2,14},{3,7},{4,52},{5,21},{6,2},{7,11},{8,56},{9,25... | collective-permute-start | bytes 786440 | tf_op jit(solution)/shard_map/ppermute | solution.py:80
  57.2 1.8 %collective-permute-start.19 = (bf16[1024,128]{1,0:T(8,128)(2,1)S(1)}, bf16[1024,128]{1,0:T(8,128)(2,1)S(1)}, u32[]{:S(2)}, u32[]{:S(2)}) collective-permute-start(bf16[1024,128]{1,0:T(8,128)(2,1)S(1)} %slice.44), channel_id=1, source_target_pairs={{0,2},{1,3},{2,0},{3,1},{4,6},{5,7},{6,4},{7,5},{8,10},{9,11},{10,... | collective-permute-start | bytes 786440 | tf_op jit(solution)/shard_map/ppermute | solution.py:80
  60.1 2.6 %collective-permute-start.22 = (bf16[1024,128]{1,0:T(8,128)(2,1)S(1)}, bf16[1024,128]{1,0:T(8,128)(2,1)S(1)}, u32[]{:S(2)}, u32[]{:S(2)}) collective-permute-start(bf16[1024,128]{1,0:T(8,128)(2,1)S(1)} %slice.37), channel_id=1, source_target_pairs={{0,4},{1,13},{2,18},{3,51},{4,8},{5,1},{6,22},{7,55},{8,12},{9,5},... | collective-permute-start | bytes 786440 | tf_op jit(solution)/shard_map/ppermute | solution.py:80
  62.6 2.9 %terms.6.refs_6_.refs_5_ = f32[2048,128]{1,0:T(8,128)S(1)} custom-call(s32[2]{0:T(128)S(1)} %pad_add_fusion.1.where, s32[3,64]{1,0:T(4,128)S(1)} %pad_add_fusion.codes, bf16[64,2,256,256]{3,2,1,0:T(8,128)(2,1)S(1)} %load.1.blocks, bf16[2048,128]{1,0:T(8,128)(2,1)S(1)} %collective-permute-done.14.refs_0_, ...), custom_call_target="tpu_custom_call" | custom-call | flops 671088640 | bytes 7864320 | tf_op jit(solution)/shard_map/terms/pallas_call | solution.py:229
  66.5 1.5 %collective-permute-done.22.refs_4_ = bf16[1024,128]{1,0:T(8,128)(2,1)S(1)} collective-permute-done((bf16[1024,128]{1,0:T(8,128)(2,1)S(1)}, bf16[1024,128]{1,0:T(8,128)(2,1)S(1)}, u32[]{:S(2)}, u32[]{:S(2)}) %collective-permute-start.22) | collective-permute-done | bytes 262176 | tf_op jit(solution)/shard_map/ppermute | solution.py:80
  68.8 1.5 %collective-permute-start.23 = (bf16[12,256,128]{2,1,0:T(8,128)(2,1)S(1)}, bf16[12,256,128]{2,1,0:T(8,128)(2,1)S(1)}, u32[]{:S(2)}, u32[]{:S(2)}) collective-permute-start(bf16[12,256,128]{2,1,0:T(8,128)(2,1)S(1)} %pack.7), channel_id=1, source_target_pairs={{0,1},{1,0},{2,3},{3,2},{4,5},{5,4},{6,7},{7,6},{8,9},{9,8},{10,11... | collective-permute-start | bytes 2359304 | tf_op jit(solution)/shard_map/ppermute | solution.py:80
  70.3 1.2 %terms.8.refs_1_ = f32[1024,128]{1,0:T(8,128)S(1)} custom-call(s32[2]{0:T(128)S(1)} %pad_add_fusion.1.where, s32[3,64]{1,0:T(4,128)S(1)} %pad_add_fusion.codes, bf16[64,2,256,256]{3,2,1,0:T(8,128)(2,1)S(1)} %load.1.blocks, bf16[2048,128]{1,0:T(8,128)(2,1)S(1)} %collective-permute-done.17.refs_0_, bf16[1024,128]{1,0:T(8,128)(2,1)S(1)} %collective-permute-done.18.refs_1_, ...), custom_call_target="tpu_custom_call" | custom-call | flops 201326592 | bytes 2359296 | tf_op jit(solution)/shard_map/terms/pallas_call | solution.py:229
  72.3 1.3 %terms.9 = f32[1024,128]{1,0:T(8,128)S(1)} custom-call(s32[2]{0:T(128)S(1)} %pad_add_fusion.1.where, s32[3,64]{1,0:T(4,128)S(1)} %pad_add_fusion.codes, bf16[64,2,256,256]{3,2,1,0:T(8,128)(2,1)S(1)} %load.1.blocks, bf16[12,256,128]{2,1,0:T(8,128)(2,1)S(1)} %collective-permute-done.23.refs_5_.refs_0_, f32[1024,128]{1,0:T(8,128)S(1)} %terms.8.refs_1_), custom_call_target="tpu_custom_call" | custom-call | flops 201326592 | bytes 2359296 | tf_op jit(solution)/shard_map/terms/pallas_call | solution.py:229
  73.6 1.3 %collective-permute-start.24 = (bf16[1024,128]{1,0:T(8,128)(2,1)S(1)}, bf16[1024,128]{1,0:T(8,128)(2,1)S(1)}, u32[]{:S(2)}, u32[]{:S(2)}) collective-permute-start(bf16[1024,128]{1,0:T(8,128)(2,1)S(1)} %convert_element_type.12), channel_id=1, source_target_pairs={{0,64},{64,0},{1,65},{65,1},{2,66},{66,2},{3,67},{67,3},{4,68},{68... | collective-permute-start | bytes 786440 | tf_op jit(solution)/shard_map/ppermute | solution.py:350
  74.9 1.9 %terms.7 = f32[1024,128]{1,0:T(8,128)S(1)} custom-call(s32[2]{0:T(128)S(1)} %pad_add_fusion.1.where, s32[3,64]{1,0:T(4,128)S(1)} %pad_add_fusion.codes, bf16[64,2,256,256]{3,2,1,0:T(8,128)(2,1)S(1)} %load.1.blocks, bf16[2048,128]{1,0:T(8,128)(2,1)S(1)} %collective-permute-done.17.refs_0_, bf16[1024,128]{1,0:T(8,128)(2,1)S(1)} %collective-permute-done.18.refs_1_, ...), custom_call_target="tpu_custom_call" | custom-call | flops 402653184 | bytes 4718592 | tf_op jit(solution)/shard_map/terms/pallas_call | solution.py:229
  76.8 3.8 %collective-permute-done.24 = bf16[1024,128]{1,0:T(8,128)(2,1)S(1)} collective-permute-done((bf16[1024,128]{1,0:T(8,128)(2,1)S(1)}, bf16[1024,128]{1,0:T(8,128)(2,1)S(1)}, u32[]{:S(2)}, u32[]{:S(2)}) %collective-permute-start.24) | collective-permute-done | bytes 262176 | tf_op jit(solution)/shard_map/ppermute | solution.py:350
  80.6 1.1 %fusion.1 = bf16[1024,256]{1,0:T(8,128)(2,1)} fusion(bf16[128,256]{1,0:T(8,128)(2,1)S(1)} %copy-done, f32[256]{0:T(256)S(1)} %copy-done.2, f32[1024,128]{1,0:T(8,128)S(1)} %terms.7, bf16[1024,128]{1,0:T(8,128)(2,1)S(1)} %collective-permute-done.24), kind=kOutput, calls=%fused_computation.2 | convolution fusion | flops 68288512 | bytes 1377280 | tf_op jit(solution)/shard_map/dot_general | solution.py:352
  (54 shorter events, 11.5 us)
Async XLA Ops:
  0.0 80.6 %copy-start = (bf16[128,256]{1,0:T(8,128)(2,1)S(1)}, bf16[128,256]{1,0:T(8,128)(2,1)}, u32[]{:S(2)}) copy-start(bf16[128,256]{1,0:T(8,128)(2,1)} %param.10) | copy-start | bytes 196612
  0.0 10.8 %collective-permute-start.2 = (bf16[1024,128]{1,0:T(8,128)(2,1)}, bf16[1024,128]{1,0:T(8,128)(2,1)S(1)}, u32[]{:S(2)}, u32[]{:S(2)}) collective-permute-start(bf16[1024,128]{1,0:T(8,128)(2,1)} %refs_0_.3), channel_id=1, source_target_pairs={{0,2},{1,3},{2,0},{3,1},{4,6},{5,7},{6,4},{7,5},{8,10},{9,11},{10,... | collective-permute-start | bytes 786440 | tf_op jit(solution)/shard_map/ppermute | solution.py:80
  3.6 9.0 %collective-permute-start.3 = (bf16[1024,128]{1,0:T(8,128)(2,1)}, bf16[1024,128]{1,0:T(8,128)(2,1)S(1)}, u32[]{:S(2)}, u32[]{:S(2)}) collective-permute-start(bf16[1024,128]{1,0:T(8,128)(2,1)} %refs_0_.3), channel_id=1, source_target_pairs={{0,4},{1,13},{2,18},{3,51},{4,8},{5,1},{6,22},{7,55},{8,12},{9,5},... | collective-permute-start | bytes 786440 | tf_op jit(solution)/shard_map/ppermute | solution.py:80
  6.3 9.9 %collective-permute-start.4 = (bf16[1024,128]{1,0:T(8,128)(2,1)}, bf16[1024,128]{1,0:T(8,128)(2,1)S(1)}, u32[]{:S(2)}, u32[]{:S(2)}) collective-permute-start(bf16[1024,128]{1,0:T(8,128)(2,1)} %refs_0_.3), channel_id=1, source_target_pairs={{0,16},{1,49},{2,6},{3,15},{4,20},{5,53},{6,10},{7,3},{8,24},{9,57... | collective-permute-start | bytes 786440 | tf_op jit(solution)/shard_map/ppermute | solution.py:80
  10.1 7.2 %collective-permute-start = (bf16[1024,128]{1,0:T(8,128)(2,1)}, bf16[1024,128]{1,0:T(8,128)(2,1)S(1)}, u32[]{:S(2)}, u32[]{:S(2)}) collective-permute-start(bf16[1024,128]{1,0:T(8,128)(2,1)} %refs_0_.3), channel_id=1, source_target_pairs={{0,48},{1,17},{2,14},{3,7},{4,52},{5,21},{6,2},{7,11},{8,56},{9,25... | collective-permute-start | bytes 786440 | tf_op jit(solution)/shard_map/ppermute | solution.py:80
  10.1 7.2 %collective-permute-start.1 = (bf16[1024,128]{1,0:T(8,128)(2,1)}, bf16[1024,128]{1,0:T(8,128)(2,1)S(1)}, u32[]{:S(2)}, u32[]{:S(2)}) collective-permute-start(bf16[1024,128]{1,0:T(8,128)(2,1)} %refs_0_.3), channel_id=1, source_target_pairs={{0,12},{1,5},{2,50},{3,19},{4,0},{5,9},{6,54},{7,23},{8,4},{9,13},... | collective-permute-start | bytes 786440 | tf_op jit(solution)/shard_map/ppermute | solution.py:80
  10.8 6.5 %collective-permute-start.5 = (s32[3,64]{1,0:T(4,128)S(1)}, s32[3,64]{1,0:T(4,128)S(1)}, u32[]{:S(2)}, u32[]{:S(2)}) collective-permute-start(s32[3,64]{1,0:T(4,128)S(1)} %pad_add_fusion.codes), channel_id=1, source_target_pairs={{0,1},{1,0},{2,3},{3,2},{4,5},{5,4},{6,7},{7,6},{8,9},{9,8},{10,11... | collective-permute-start | bytes 2312 | tf_op jit(solution)/shard_map/ppermute | solution.py:80
  17.3 12.7 %collective-permute-start.10 = (bf16[2048,128]{1,0:T(8,128)(2,1)}, bf16[2048,128]{1,0:T(8,128)(2,1)S(1)}, u32[]{:S(2)}, u32[]{:S(2)}) collective-permute-start(bf16[2048,128]{1,0:T(8,128)(2,1)} %get-tuple-element.39), channel_id=1, source_target_pairs={{0,4},{1,13},{2,18},{3,51},{4,8},{5,1},{6,22},{7,55},{8,12},{9,5},... | collective-permute-start | bytes 1572872 | tf_op jit(solution)/shard_map/ppermute | solution.py:80
  18.5 12.8 %collective-permute-start.9 = (bf16[2048,128]{1,0:T(8,128)(2,1)}, bf16[2048,128]{1,0:T(8,128)(2,1)S(1)}, u32[]{:S(2)}, u32[]{:S(2)}) collective-permute-start(bf16[2048,128]{1,0:T(8,128)(2,1)} %get-tuple-element.38), channel_id=1, source_target_pairs={{0,48},{1,17},{2,14},{3,7},{4,52},{5,21},{6,2},{7,11},{8,56},{9,25... | collective-permute-start | bytes 1572872 | tf_op jit(solution)/shard_map/ppermute | solution.py:80
  18.6 12.9 %collective-permute-start.8 = (bf16[2048,128]{1,0:T(8,128)(2,1)S(1)}, bf16[2048,128]{1,0:T(8,128)(2,1)S(1)}, u32[]{:S(2)}, u32[]{:S(2)}) collective-permute-start(bf16[2048,128]{1,0:T(8,128)(2,1)S(1)} %constant_dynamic-update-slice_fusion.2.refs_2_), channel_id=1, source_target_pairs={{0,2},{1,3},{2,0},{3,1},{4,6},{5,7},{6,4},{7,5},{8,10},{9,11},{10,... | collective-permute-start | bytes 1572872 | tf_op jit(solution)/shard_map/ppermute | solution.py:80
  20.4 13.7 %collective-permute-start.7 = (bf16[2048,128]{1,0:T(8,128)(2,1)S(1)}, bf16[2048,128]{1,0:T(8,128)(2,1)}, u32[]{:S(2)}, u32[]{:S(2)}) collective-permute-start(bf16[2048,128]{1,0:T(8,128)(2,1)S(1)} %constant_dynamic-update-slice_fusion.refs_1_), channel_id=1, source_target_pairs={{0,16},{1,49},{2,6},{3,15},{4,20},{5,53},{6,10},{7,3},{8,24},{9,57... | collective-permute-start | bytes 1572872 | tf_op jit(solution)/shard_map/ppermute | solution.py:80
  22.3 11.7 %collective-permute-start.6 = (bf16[2048,128]{1,0:T(8,128)(2,1)}, bf16[2048,128]{1,0:T(8,128)(2,1)S(1)}, u32[]{:S(2)}, u32[]{:S(2)}) collective-permute-start(bf16[2048,128]{1,0:T(8,128)(2,1)} %pad_maximum_fusion), channel_id=1, source_target_pairs={{0,12},{1,5},{2,50},{3,19},{4,0},{5,9},{6,54},{7,23},{8,4},{9,13},... | collective-permute-start | bytes 1572872 | tf_op jit(solution)/shard_map/ppermute | solution.py:80
  23.3 5.9 %copy-start.1 = (bf16[1024,128]{1,0:T(8,128)(2,1)S(1)}, bf16[1024,128]{1,0:T(8,128)(2,1)}, u32[]{:S(2)}) copy-start(bf16[1024,128]{1,0:T(8,128)(2,1)} %refs_0_.3) | copy-start | bytes 786436
  35.6 4.5 %collective-permute-start.12 = (bf16[32,256,128]{2,1,0:T(8,128)(2,1)S(1)}, bf16[32,256,128]{2,1,0:T(8,128)(2,1)S(1)}, u32[]{:S(2)}, u32[]{:S(2)}) collective-permute-start(bf16[32,256,128]{2,1,0:T(8,128)(2,1)S(1)} %pack.5), channel_id=1, source_target_pairs={{0,1},{1,0},{2,3},{3,2},{4,5},{5,4},{6,7},{7,6},{8,9},{9,8},{10,11... | collective-permute-start | bytes 6291464 | tf_op jit(solution)/shard_map/ppermute | solution.py:80
  36.4 11.6 %collective-permute-start.15 = (bf16[2048,128]{1,0:T(8,128)(2,1)S(1)}, bf16[2048,128]{1,0:T(8,128)(2,1)S(1)}, u32[]{:S(2)}, u32[]{:S(2)}) collective-permute-start(bf16[2048,128]{1,0:T(8,128)(2,1)S(1)} %pad_maximum_fusion.5), channel_id=1, source_target_pairs={{0,48},{1,17},{2,14},{3,7},{4,52},{5,21},{6,2},{7,11},{8,56},{9,25... | collective-permute-start | bytes 1572872 | tf_op jit(solution)/shard_map/ppermute | solution.py:80
  37.4 10.6 %collective-permute-start.14 = (bf16[2048,128]{1,0:T(8,128)(2,1)S(1)}, bf16[2048,128]{1,0:T(8,128)(2,1)S(1)}, u32[]{:S(2)}, u32[]{:S(2)}) collective-permute-start(bf16[2048,128]{1,0:T(8,128)(2,1)S(1)} %pad_maximum_fusion.4), channel_id=1, source_target_pairs={{0,4},{1,13},{2,18},{3,51},{4,8},{5,1},{6,22},{7,55},{8,12},{9,5},... | collective-permute-start | bytes 1572872 | tf_op jit(solution)/shard_map/ppermute | solution.py:80
  37.8 12.1 %collective-permute-start.11 = (bf16[2048,128]{1,0:T(8,128)(2,1)S(1)}, bf16[2048,128]{1,0:T(8,128)(2,1)S(1)}, u32[]{:S(2)}, u32[]{:S(2)}) collective-permute-start(bf16[2048,128]{1,0:T(8,128)(2,1)S(1)} %collective-permute-done.6.refs_1_.refs_5_), channel_id=1, source_target_pairs={{0,2},{1,3},{2,0},{3,1},{4,6},{5,7},{6,4},{7,5},{8,10},{9,11},{10,... | collective-permute-start | bytes 1572872 | tf_op jit(solution)/shard_map/ppermute | solution.py:80
  40.1 10.8 %collective-permute-start.16 = (bf16[2048,128]{1,0:T(8,128)(2,1)S(1)}, bf16[2048,128]{1,0:T(8,128)(2,1)S(1)}, u32[]{:S(2)}, u32[]{:S(2)}) collective-permute-start(bf16[2048,128]{1,0:T(8,128)(2,1)S(1)} %collective-permute-done.10.refs_4_.refs_8_), channel_id=1, source_target_pairs={{0,16},{1,49},{2,6},{3,15},{4,20},{5,53},{6,10},{7,3},{8,24},{9,57... | collective-permute-start | bytes 1572872 | tf_op jit(solution)/shard_map/ppermute | solution.py:80
  42.2 12.2 %collective-permute-start.13 = (bf16[2048,128]{1,0:T(8,128)(2,1)S(1)}, bf16[2048,128]{1,0:T(8,128)(2,1)S(1)}, u32[]{:S(2)}, u32[]{:S(2)}) collective-permute-start(bf16[2048,128]{1,0:T(8,128)(2,1)S(1)} %collective-permute-done.8.refs_2_.refs_6_), channel_id=1, source_target_pairs={{0,12},{1,5},{2,50},{3,19},{4,0},{5,9},{6,54},{7,23},{8,4},{9,13},... | collective-permute-start | bytes 1572872 | tf_op jit(solution)/shard_map/ppermute | solution.py:80
  55.5 4.6 %collective-permute-start.21 = (bf16[20,256,128]{2,1,0:T(8,128)(2,1)S(1)}, bf16[20,256,128]{2,1,0:T(8,128)(2,1)S(1)}, u32[]{:S(2)}, u32[]{:S(2)}) collective-permute-start(bf16[20,256,128]{2,1,0:T(8,128)(2,1)S(1)} %pack.6), channel_id=1, source_target_pairs={{0,1},{1,0},{2,3},{3,2},{4,5},{5,4},{6,7},{7,6},{8,9},{9,8},{10,11... | collective-permute-start | bytes 3932168 | tf_op jit(solution)/shard_map/ppermute | solution.py:80
  55.7 10.9 %collective-permute-start.17 = (bf16[2048,128]{1,0:T(8,128)(2,1)S(1)}, bf16[2048,128]{1,0:T(8,128)(2,1)S(1)}, u32[]{:S(2)}, u32[]{:S(2)}) collective-permute-start(bf16[2048,128]{1,0:T(8,128)(2,1)S(1)} %pad_maximum_fusion.3), channel_id=1, source_target_pairs={{0,12},{1,5},{2,50},{3,19},{4,0},{5,9},{6,54},{7,23},{8,4},{9,13},... | collective-permute-start | bytes 1572872 | tf_op jit(solution)/shard_map/ppermute | solution.py:80
  56.2 9.3 %collective-permute-start.20 = (bf16[1024,128]{1,0:T(8,128)(2,1)S(1)}, bf16[1024,128]{1,0:T(8,128)(2,1)S(1)}, u32[]{:S(2)}, u32[]{:S(2)}) collective-permute-start(bf16[1024,128]{1,0:T(8,128)(2,1)S(1)} %slice.45), channel_id=1, source_target_pairs={{0,48},{1,17},{2,14},{3,7},{4,52},{5,21},{6,2},{7,11},{8,56},{9,25... | collective-permute-start | bytes 786440 | tf_op jit(solution)/shard_map/ppermute | solution.py:80
  57.2 8.3 %collective-permute-start.19 = (bf16[1024,128]{1,0:T(8,128)(2,1)S(1)}, bf16[1024,128]{1,0:T(8,128)(2,1)S(1)}, u32[]{:S(2)}, u32[]{:S(2)}) collective-permute-start(bf16[1024,128]{1,0:T(8,128)(2,1)S(1)} %slice.44), channel_id=1, source_target_pairs={{0,2},{1,3},{2,0},{3,1},{4,6},{5,7},{6,4},{7,5},{8,10},{9,11},{10,... | collective-permute-start | bytes 786440 | tf_op jit(solution)/shard_map/ppermute | solution.py:80
  59.0 7.5 %collective-permute-start.18 = (bf16[1024,128]{1,0:T(8,128)(2,1)S(1)}, bf16[1024,128]{1,0:T(8,128)(2,1)S(1)}, u32[]{:S(2)}, u32[]{:S(2)}) collective-permute-start(bf16[1024,128]{1,0:T(8,128)(2,1)S(1)} %get-tuple-element.56), channel_id=1, source_target_pairs={{0,32},{1,33},{2,10},{3,11},{4,36},{5,37},{6,14},{7,15},{8,40},{9,... | collective-permute-start | bytes 786440 | tf_op jit(solution)/shard_map/ppermute | solution.py:80
  60.1 7.9 %collective-permute-start.22 = (bf16[1024,128]{1,0:T(8,128)(2,1)S(1)}, bf16[1024,128]{1,0:T(8,128)(2,1)S(1)}, u32[]{:S(2)}, u32[]{:S(2)}) collective-permute-start(bf16[1024,128]{1,0:T(8,128)(2,1)S(1)} %slice.37), channel_id=1, source_target_pairs={{0,4},{1,13},{2,18},{3,51},{4,8},{5,1},{6,22},{7,55},{8,12},{9,5},... | collective-permute-start | bytes 786440 | tf_op jit(solution)/shard_map/ppermute | solution.py:80
  68.8 3.4 %collective-permute-start.23 = (bf16[12,256,128]{2,1,0:T(8,128)(2,1)S(1)}, bf16[12,256,128]{2,1,0:T(8,128)(2,1)S(1)}, u32[]{:S(2)}, u32[]{:S(2)}) collective-permute-start(bf16[12,256,128]{2,1,0:T(8,128)(2,1)S(1)} %pack.7), channel_id=1, source_target_pairs={{0,1},{1,0},{2,3},{3,2},{4,5},{5,4},{6,7},{7,6},{8,9},{9,8},{10,11... | collective-permute-start | bytes 2359304 | tf_op jit(solution)/shard_map/ppermute | solution.py:80
  73.6 7.0 %copy-start.2 = (f32[256]{0:T(256)S(1)}, f32[256]{0:T(256)}, u32[]{:S(2)}) copy-start(f32[256]{0:T(256)} %param.11) | copy-start | bytes 3076
  73.6 7.0 %collective-permute-start.24 = (bf16[1024,128]{1,0:T(8,128)(2,1)S(1)}, bf16[1024,128]{1,0:T(8,128)(2,1)S(1)}, u32[]{:S(2)}, u32[]{:S(2)}) collective-permute-start(bf16[1024,128]{1,0:T(8,128)(2,1)S(1)} %convert_element_type.12), channel_id=1, source_target_pairs={{0,64},{64,0},{1,65},{65,1},{2,66},{66,2},{3,67},{67,3},{4,68},{68... | collective-permute-start | bytes 786440 | tf_op jit(solution)/shard_map/ppermute | solution.py:350

commit v3 on v2

--- a/solution.py
+++ b/solution.py
@@ -142,9 +142,7 @@
         owners[n] = owner_of(where, unit, flip)
     if total_in is None:
         total[...] = jnp.zeros_like(total)
-    elif total_in.shape == total.shape:
-        total[...] = total_in[...]
-    else:
+    elif total_in.shape != total.shape:
         total[...] = total_in[half * size : (half + 1) * size, :]
 
     def target_of(owner, k):
@@ -226,11 +224,14 @@
     n = sum(len(us) for us, _ in layout) * SLOTS
     vmem = pl.BlockSpec(memory_space=pltpu.VMEM)
     operands = [where, codes, blocks] + [x for x, _, _ in sources] + ([] if running is None else [running])
+    shape = (8 * block if half is None else 4 * block, channels)
+    same = running is not None and running.shape == shape
     return pl.pallas_call(
         functools.partial(terms_kernel, layout, half),
-        out_shape=jax.ShapeDtypeStruct((8 * block if half is None else 4 * block, channels), jnp.float32),
+        out_shape=jax.ShapeDtypeStruct(shape, jnp.float32),
         in_specs=[pl.BlockSpec(memory_space=pltpu.SMEM)] * 2 + [vmem] * (len(operands) - 2),
         out_specs=vmem,
+        input_output_aliases={len(operands) - 1: 0} if same else {},
         scratch_shapes=[pltpu.SMEM((n // SLOTS,), jnp.int32)],
         compiler_params=pltpu.CompilerParams(vmem_limit_bytes=VMEM_LIMIT),
         cost_estimate=pl.CostEstimate(

time: 82.9 us -> 82.5 us (level)
  Pallas kernels: 21.7 us -> 19.4 us
  waiting for transfers between devices: 21.5 us -> 23.8 us
    pallas_call x5, Pallas kernels: 11.8 us -> 9.84 us  [terms(): pl.pallas_call(functools.partial(terms_kernel, layout, half), out_shape=j...]
    ppermute x24, waiting for transfers between devices: 17.7 us -> 19.3 us  [send(): return lax.ppermute(x, 'row', pairs_of(channel))]
  transfers between devices with their start and end apart: 25 -> 25, of which waited for: 12 -> 13; matrix products, arithmetic and copies ran while one was open for 4% -> 4% of each run, Pallas kernels for 21% -> 19%
where the time goes in v3:
time: 82.5 us; the launch traced here: 82 us
  starting transfers between devices  34.3 us (42%)
  waiting for transfers between devices  23.8 us (29%)
  Pallas kernels  19.4 us (24%)
  other arithmetic  2.79 us (3%)
  matrix products  1.08 us (1%)
    ppermute x24, starting transfers between devices, send(): return lax.ppermute(x, 'row', pairs_of(channel))  33.1 us
    ppermute x24, waiting for transfers between devices, send(): return lax.ppermute(x, 'row', pairs_of(channel))  19.3 us
    pallas_call x5, Pallas kernels, terms(): pl.pallas_call(functools.partial(terms_kernel, layout, half), out_shape=j...  9.84 us
    pallas_call x1, Pallas kernels, load(): pl.pallas_call(load_kernel, out_shape=pltpu.VMEM(blocks.shape, blocks.dty...  5.82 us
    ppermute x1, waiting for transfers between devices, body(): received = lax.ppermute(sent.astype(jnp.bfloat16), 'rep', [(0, 1), (1, 0)])  4.58 us
    pallas_call x4, Pallas kernels, pack(): pl.pallas_call(functools.partial(pack_kernel, layout, 0 if into is None e...  3.76 us
    concatenate x5, other arithmetic, payload(): return (x[0] if len(x) == 1 else jnp.concatenate(x), units)  1.98 us
  transfers between devices with their start and end apart: 25, of which 13 were waited for; matrix products, arithmetic and copies ran while one was open for 4% of the time, Pallas kernels for 19%

profile of v3, /device:TPU:1, one launch (start us, length us, event | category | flops | bytes accessed | tf_op | source)
XLA Modules:
  0.0 82.0 jit_solution(6946743011625786562)
XLA Ops:
  0.0 3.6 %collective-permute-start.2 = (bf16[1024,128]{1,0:T(8,128)(2,1)}, bf16[1024,128]{1,0:T(8,128)(2,1)S(1)}, u32[]{:S(2)}, u32[]{:S(2)}) collective-permute-start(bf16[1024,128]{1,0:T(8,128)(2,1)} %refs_0_.3), channel_id=1, source_target_pairs={{0,2},{1,3},{2,0},{3,1},{4,6},{5,7},{6,4},{7,5},{8,10},{9,11},{10,... | collective-permute-start | bytes 786440 | tf_op jit(solution)/shard_map/ppermute | solution.py:80
  3.6 2.7 %collective-permute-start.3 = (bf16[1024,128]{1,0:T(8,128)(2,1)}, bf16[1024,128]{1,0:T(8,128)(2,1)S(1)}, u32[]{:S(2)}, u32[]{:S(2)}) collective-permute-start(bf16[1024,128]{1,0:T(8,128)(2,1)} %refs_0_.3), channel_id=1, source_target_pairs={{0,4},{1,13},{2,18},{3,51},{4,8},{5,1},{6,22},{7,55},{8,12},{9,5},... | collective-permute-start | bytes 786440 | tf_op jit(solution)/shard_map/ppermute | solution.py:80
  6.3 3.8 %collective-permute-start.4 = (bf16[1024,128]{1,0:T(8,128)(2,1)}, bf16[1024,128]{1,0:T(8,128)(2,1)S(1)}, u32[]{:S(2)}, u32[]{:S(2)}) collective-permute-start(bf16[1024,128]{1,0:T(8,128)(2,1)} %refs_0_.3), channel_id=1, source_target_pairs={{0,16},{1,49},{2,6},{3,15},{4,20},{5,53},{6,10},{7,3},{8,24},{9,57... | collective-permute-start | bytes 786440 | tf_op jit(solution)/shard_map/ppermute | solution.py:80
  10.8 1.8 %collective-permute-start.5 = (s32[3,64]{1,0:T(4,128)S(1)}, s32[3,64]{1,0:T(4,128)S(1)}, u32[]{:S(2)}, u32[]{:S(2)}) collective-permute-start(s32[3,64]{1,0:T(4,128)S(1)} %pad_add_fusion.codes), channel_id=1, source_target_pairs={{0,1},{1,0},{2,3},{3,2},{4,5},{5,4},{6,7},{7,6},{8,9},{9,8},{10,11... | collective-permute-start | bytes 2312 | tf_op jit(solution)/shard_map/ppermute | solution.py:80
  12.6 3.6 %collective-permute-done.4 = bf16[1024,128]{1,0:T(8,128)(2,1)S(1)} collective-permute-done((bf16[1024,128]{1,0:T(8,128)(2,1)}, bf16[1024,128]{1,0:T(8,128)(2,1)S(1)}, u32[]{:S(2)}, u32[]{:S(2)}) %collective-permute-start.4) | collective-permute-done | bytes 262176 | tf_op jit(solution)/shard_map/ppermute | solution.py:80
  16.2 1.0 %pad_maximum_fusion.2 = (bf16[2048,128]{1,0:T(8,128)(2,1)}, bf16[2048,128]{1,0:T(8,128)(2,1)}) fusion(bf16[1024,128]{1,0:T(8,128)(2,1)S(1)} %collective-permute-done.2.refs_3_, bf16[1024,128]{1,0:T(8,128)(2,1)S(1)} %collective-permute-done.4, bf16[1024,128]{1,0:T(8,128)(2,1)S(1)} %collective-permute-done.3), kind=kLoop, calls=%fused_computation.5 | loop fusion | flops 2097152 | bytes 1835008 | tf_op jit(solution)/shard_map/concatenate | solution.py:284
  17.3 1.2 %collective-permute-start.10 = (bf16[2048,128]{1,0:T(8,128)(2,1)}, bf16[2048,128]{1,0:T(8,128)(2,1)S(1)}, u32[]{:S(2)}, u32[]{:S(2)}) collective-permute-start(bf16[2048,128]{1,0:T(8,128)(2,1)} %get-tuple-element.39), channel_id=1, source_target_pairs={{0,4},{1,13},{2,18},{3,51},{4,8},{5,1},{6,22},{7,55},{8,12},{9,5},... | collective-permute-start | bytes 1572872 | tf_op jit(solution)/shard_map/ppermute | solution.py:80
  18.6 1.7 %collective-permute-start.8 = (bf16[2048,128]{1,0:T(8,128)(2,1)S(1)}, bf16[2048,128]{1,0:T(8,128)(2,1)S(1)}, u32[]{:S(2)}, u32[]{:S(2)}) collective-permute-start(bf16[2048,128]{1,0:T(8,128)(2,1)S(1)} %constant_dynamic-update-slice_fusion.2.refs_2_), channel_id=1, source_target_pairs={{0,2},{1,3},{2,0},{3,1},{4,6},{5,7},{6,4},{7,5},{8,10},{9,11},{10,... | collective-permute-start | bytes 1572872 | tf_op jit(solution)/shard_map/ppermute | solution.py:80
  20.4 1.1 %collective-permute-start.7 = (bf16[2048,128]{1,0:T(8,128)(2,1)S(1)}, bf16[2048,128]{1,0:T(8,128)(2,1)}, u32[]{:S(2)}, u32[]{:S(2)}) collective-permute-start(bf16[2048,128]{1,0:T(8,128)(2,1)S(1)} %constant_dynamic-update-slice_fusion.refs_1_), channel_id=1, source_target_pairs={{0,16},{1,49},{2,6},{3,15},{4,20},{5,53},{6,10},{7,3},{8,24},{9,57... | collective-permute-start | bytes 1572872 | tf_op jit(solution)/shard_map/ppermute | solution.py:80
  23.3 5.8 %load.1.blocks = bf16[64,2,256,256]{3,2,1,0:T(8,128)(2,1)S(1)} custom-call(bf16[64,2,256,256]{3,2,1,0:T(8,128)(2,1)} %bitcast.8), custom_call_target="tpu_custom_call" | custom-call | bytes 16777216 | tf_op jit(solution)/shard_map/load/pallas_call | solution.py:253
  30.0 1.4 %collective-permute-done.9.refs_3_.refs_7_ = bf16[2048,128]{1,0:T(8,128)(2,1)S(1)} collective-permute-done((bf16[2048,128]{1,0:T(8,128)(2,1)}, bf16[2048,128]{1,0:T(8,128)(2,1)S(1)}, u32[]{:S(2)}, u32[]{:S(2)}) %collective-permute-start.9) | collective-permute-done | bytes 524320 | tf_op jit(solution)/shard_map/ppermute | solution.py:80
  31.5 2.5 %collective-permute-done.7.refs_0_.refs_4_ = bf16[2048,128]{1,0:T(8,128)(2,1)} collective-permute-done((bf16[2048,128]{1,0:T(8,128)(2,1)S(1)}, bf16[2048,128]{1,0:T(8,128)(2,1)}, u32[]{:S(2)}, u32[]{:S(2)}) %collective-permute-start.7) | collective-permute-done | bytes 524320 | tf_op jit(solution)/shard_map/ppermute | solution.py:80
  34.1 1.4 %pack.5 = bf16[32,256,128]{2,1,0:T(8,128)(2,1)S(1)} custom-call(s32[2]{0:T(128)S(1)} %pad_add_fusion.1.where, s32[3,64]{1,0:T(4,128)S(1)} %collective-permute-done.5.codes, bf16[2048,128]{1,0:T(8,128)(2,1)} %collective-permute-done.7.refs_0_.refs_4_, bf16[2048,128]{1,0:T(8,128)(2,1)S(1)} %collective-permute-done.6.refs_1_.refs_5_, ...), custom_call_target="tpu_custom_call", output_to_operand_aliasing={{}: (7, {})} | custom-call | bytes 2621440 | tf_op jit(solution)/shard_map/pack/pallas_call | solution.py:117
  37.9 1.9 %collective-permute-start.11 = (bf16[2048,128]{1,0:T(8,128)(2,1)S(1)}, bf16[2048,128]{1,0:T(8,128)(2,1)S(1)}, u32[]{:S(2)}, u32[]{:S(2)}) collective-permute-start(bf16[2048,128]{1,0:T(8,128)(2,1)S(1)} %collective-permute-done.6.refs_1_.refs_5_), channel_id=1, source_target_pairs={{0,2},{1,3},{2,0},{3,1},{4,6},{5,7},{6,4},{7,5},{8,10},{9,11},{10,... | collective-permute-start | bytes 1572872 | tf_op jit(solution)/shard_map/ppermute | solution.py:80
  40.1 2.2 %collective-permute-start.16 = (bf16[2048,128]{1,0:T(8,128)(2,1)S(1)}, bf16[2048,128]{1,0:T(8,128)(2,1)S(1)}, u32[]{:S(2)}, u32[]{:S(2)}) collective-permute-start(bf16[2048,128]{1,0:T(8,128)(2,1)S(1)} %collective-permute-done.10.refs_4_.refs_8_), channel_id=1, source_target_pairs={{0,16},{1,49},{2,6},{3,15},{4,20},{5,53},{6,10},{7,3},{8,24},{9,57... | collective-permute-start | bytes 1572872 | tf_op jit(solution)/shard_map/ppermute | solution.py:80
  42.3 1.2 %collective-permute-start.13 = (bf16[2048,128]{1,0:T(8,128)(2,1)S(1)}, bf16[2048,128]{1,0:T(8,128)(2,1)S(1)}, u32[]{:S(2)}, u32[]{:S(2)}) collective-permute-start(bf16[2048,128]{1,0:T(8,128)(2,1)S(1)} %collective-permute-done.8.refs_2_.refs_6_), channel_id=1, source_target_pairs={{0,12},{1,5},{2,50},{3,19},{4,0},{5,9},{6,54},{7,23},{8,4},{9,13},... | collective-permute-start | bytes 1572872 | tf_op jit(solution)/shard_map/ppermute | solution.py:80
  43.5 3.8 %terms.5.refs_6_ = f32[2048,128]{1,0:T(8,128)S(1)} custom-call(s32[2]{0:T(128)S(1)} %pad_add_fusion.1.where, s32[3,64]{1,0:T(4,128)S(1)} %pad_add_fusion.codes, bf16[64,2,256,256]{3,2,1,0:T(8,128)(2,1)S(1)} %load.1.blocks, bf16[1024,128]{1,0:T(8,128)(2,1)S(1)} %copy-done.1, bf16[2048,128]{1,0:T(8,128)(2,1)S(1)} %constant_dynamic-update-slice_fusion.refs_1_, ...), custom_call_target="tpu_custom_call" | custom-call | flops 1073741824 | bytes 12582912 | tf_op jit(solution)/shard_map/terms/pallas_call | solution.py:229
  47.3 2.7 %collective-permute-done.11.refs_1_ = bf16[2048,128]{1,0:T(8,128)(2,1)S(1)} collective-permute-done((bf16[2048,128]{1,0:T(8,128)(2,1)S(1)}, bf16[2048,128]{1,0:T(8,128)(2,1)S(1)}, u32[]{:S(2)}, u32[]{:S(2)}) %collective-permute-start.11) | collective-permute-done | bytes 524320 | tf_op jit(solution)/shard_map/ppermute | solution.py:80
  51.0 3.5 %collective-permute-done.13.refs_3_ = bf16[2048,128]{1,0:T(8,128)(2,1)S(1)} collective-permute-done((bf16[2048,128]{1,0:T(8,128)(2,1)S(1)}, bf16[2048,128]{1,0:T(8,128)(2,1)S(1)}, u32[]{:S(2)}, u32[]{:S(2)}) %collective-permute-start.13) | collective-permute-done | bytes 524320 | tf_op jit(solution)/shard_map/ppermute | solution.py:80
  56.0 1.4 %collective-permute-start.20 = (bf16[1024,128]{1,0:T(8,128)(2,1)S(1)}, bf16[1024,128]{1,0:T(8,128)(2,1)S(1)}, u32[]{:S(2)}, u32[]{:S(2)}) collective-permute-start(bf16[1024,128]{1,0:T(8,128)(2,1)S(1)} %slice.45), channel_id=1, source_target_pairs={{0,48},{1,17},{2,14},{3,7},{4,52},{5,21},{6,2},{7,11},{8,56},{9,25... | collective-permute-start | bytes 786440 | tf_op jit(solution)/shard_map/ppermute | solution.py:80
  57.5 1.8 %collective-permute-start.19 = (bf16[1024,128]{1,0:T(8,128)(2,1)S(1)}, bf16[1024,128]{1,0:T(8,128)(2,1)S(1)}, u32[]{:S(2)}, u32[]{:S(2)}) collective-permute-start(bf16[1024,128]{1,0:T(8,128)(2,1)S(1)} %slice.44), channel_id=1, source_target_pairs={{0,2},{1,3},{2,0},{3,1},{4,6},{5,7},{6,4},{7,5},{8,10},{9,11},{10,... | collective-permute-start | bytes 786440 | tf_op jit(solution)/shard_map/ppermute | solution.py:80
  60.1 2.6 %collective-permute-start.22 = (bf16[1024,128]{1,0:T(8,128)(2,1)S(1)}, bf16[1024,128]{1,0:T(8,128)(2,1)S(1)}, u32[]{:S(2)}, u32[]{:S(2)}) collective-permute-start(bf16[1024,128]{1,0:T(8,128)(2,1)S(1)} %slice.37), channel_id=1, source_target_pairs={{0,4},{1,13},{2,18},{3,51},{4,8},{5,1},{6,22},{7,55},{8,12},{9,5},... | collective-permute-start | bytes 786440 | tf_op jit(solution)/shard_map/ppermute | solution.py:80
  62.7 2.0 %terms.6.refs_6_.refs_5_ = f32[2048,128]{1,0:T(8,128)S(1)} custom-call(s32[2]{0:T(128)S(1)} %pad_add_fusion.1.where, s32[3,64]{1,0:T(4,128)S(1)} %pad_add_fusion.codes, bf16[64,2,256,256]{3,2,1,0:T(8,128)(2,1)S(1)} %load.1.blocks, bf16[2048,128]{1,0:T(8,128)(2,1)S(1)} %collective-permute-done.14.refs_0_, ...), custom_call_target="tpu_custom_call", output_to_operand_aliasing={{}: (9, {})} | custom-call | flops 671088640 | bytes 7864320 | tf_op jit(solution)/shard_map/terms/pallas_call | solution.py:229
  65.4 1.6 %collective-permute-done.18.refs_1_ = bf16[1024,128]{1,0:T(8,128)(2,1)S(1)} collective-permute-done((bf16[1024,128]{1,0:T(8,128)(2,1)S(1)}, bf16[1024,128]{1,0:T(8,128)(2,1)S(1)}, u32[]{:S(2)}, u32[]{:S(2)}) %collective-permute-start.18) | collective-permute-done | bytes 262176 | tf_op jit(solution)/shard_map/ppermute | solution.py:80
  67.0 1.0 %collective-permute-done.22.refs_4_ = bf16[1024,128]{1,0:T(8,128)(2,1)S(1)} collective-permute-done((bf16[1024,128]{1,0:T(8,128)(2,1)S(1)}, bf16[1024,128]{1,0:T(8,128)(2,1)S(1)}, u32[]{:S(2)}, u32[]{:S(2)}) %collective-permute-start.22) | collective-permute-done | bytes 262176 | tf_op jit(solution)/shard_map/ppermute | solution.py:80
  68.7 1.6 %collective-permute-start.23 = (bf16[12,256,128]{2,1,0:T(8,128)(2,1)S(1)}, bf16[12,256,128]{2,1,0:T(8,128)(2,1)S(1)}, u32[]{:S(2)}, u32[]{:S(2)}) collective-permute-start(bf16[12,256,128]{2,1,0:T(8,128)(2,1)S(1)} %pack.7), channel_id=1, source_target_pairs={{0,1},{1,0},{2,3},{3,2},{4,5},{5,4},{6,7},{7,6},{8,9},{9,8},{10,11... | collective-permute-start | bytes 2359304 | tf_op jit(solution)/shard_map/ppermute | solution.py:80
  70.4 1.2 %terms.8.refs_1_ = f32[1024,128]{1,0:T(8,128)S(1)} custom-call(s32[2]{0:T(128)S(1)} %pad_add_fusion.1.where, s32[3,64]{1,0:T(4,128)S(1)} %pad_add_fusion.codes, bf16[64,2,256,256]{3,2,1,0:T(8,128)(2,1)S(1)} %load.1.blocks, bf16[2048,128]{1,0:T(8,128)(2,1)S(1)} %collective-permute-done.17.refs_0_, bf16[1024,128]{1,0:T(8,128)(2,1)S(1)} %collective-permute-done.18.refs_1_, ...), custom_call_target="tpu_custom_call" | custom-call | flops 201326592 | bytes 2359296 | tf_op jit(solution)/shard_map/terms/pallas_call | solution.py:229
  72.3 1.1 %terms.9 = f32[1024,128]{1,0:T(8,128)S(1)} custom-call(s32[2]{0:T(128)S(1)} %pad_add_fusion.1.where, s32[3,64]{1,0:T(4,128)S(1)} %pad_add_fusion.codes, bf16[64,2,256,256]{3,2,1,0:T(8,128)(2,1)S(1)} %load.1.blocks, bf16[12,256,128]{2,1,0:T(8,128)(2,1)S(1)} %collective-permute-done.23.refs_5_.refs_0_, ...), custom_call_target="tpu_custom_call", output_to_operand_aliasing={{}: (4, {})} | custom-call | flops 201326592 | bytes 2359296 | tf_op jit(solution)/shard_map/terms/pallas_call | solution.py:229
  73.4 1.2 %collective-permute-start.24 = (bf16[1024,128]{1,0:T(8,128)(2,1)S(1)}, bf16[1024,128]{1,0:T(8,128)(2,1)S(1)}, u32[]{:S(2)}, u32[]{:S(2)}) collective-permute-start(bf16[1024,128]{1,0:T(8,128)(2,1)S(1)} %convert_element_type.12), channel_id=1, source_target_pairs={{0,64},{64,0},{1,65},{65,1},{2,66},{66,2},{3,67},{67,3},{4,68},{68... | collective-permute-start | bytes 786440 | tf_op jit(solution)/shard_map/ppermute | solution.py:351
  74.6 1.7 %terms.7 = f32[1024,128]{1,0:T(8,128)S(1)} custom-call(s32[2]{0:T(128)S(1)} %pad_add_fusion.1.where, s32[3,64]{1,0:T(4,128)S(1)} %pad_add_fusion.codes, bf16[64,2,256,256]{3,2,1,0:T(8,128)(2,1)S(1)} %load.1.blocks, bf16[2048,128]{1,0:T(8,128)(2,1)S(1)} %collective-permute-done.17.refs_0_, bf16[1024,128]{1,0:T(8,128)(2,1)S(1)} %collective-permute-done.18.refs_1_, ...), custom_call_target="tpu_custom_call" | custom-call | flops 402653184 | bytes 4718592 | tf_op jit(solution)/shard_map/terms/pallas_call | solution.py:229
  76.3 4.6 %collective-permute-done.24 = bf16[1024,128]{1,0:T(8,128)(2,1)S(1)} collective-permute-done((bf16[1024,128]{1,0:T(8,128)(2,1)S(1)}, bf16[1024,128]{1,0:T(8,128)(2,1)S(1)}, u32[]{:S(2)}, u32[]{:S(2)}) %collective-permute-start.24) | collective-permute-done | bytes 262176 | tf_op jit(solution)/shard_map/ppermute | solution.py:351
  80.9 1.1 %fusion.1 = bf16[1024,256]{1,0:T(8,128)(2,1)} fusion(bf16[128,256]{1,0:T(8,128)(2,1)S(1)} %copy-done, f32[256]{0:T(256)S(1)} %copy-done.2, f32[1024,128]{1,0:T(8,128)S(1)} %terms.7, bf16[1024,128]{1,0:T(8,128)(2,1)S(1)} %collective-permute-done.24), kind=kOutput, calls=%fused_computation.2 | convolution fusion | flops 68288512 | bytes 1377280 | tf_op jit(solution)/shard_map/dot_general | solution.py:353
  (54 shorter events, 11.8 us)
Async XLA Ops:
  0.0 80.9 %copy-start = (bf16[128,256]{1,0:T(8,128)(2,1)S(1)}, bf16[128,256]{1,0:T(8,128)(2,1)}, u32[]{:S(2)}) copy-start(bf16[128,256]{1,0:T(8,128)(2,1)} %param.10) | copy-start | bytes 196612
  0.0 10.8 %collective-permute-start.2 = (bf16[1024,128]{1,0:T(8,128)(2,1)}, bf16[1024,128]{1,0:T(8,128)(2,1)S(1)}, u32[]{:S(2)}, u32[]{:S(2)}) collective-permute-start(bf16[1024,128]{1,0:T(8,128)(2,1)} %refs_0_.3), channel_id=1, source_target_pairs={{0,2},{1,3},{2,0},{3,1},{4,6},{5,7},{6,4},{7,5},{8,10},{9,11},{10,... | collective-permute-start | bytes 786440 | tf_op jit(solution)/shard_map/ppermute | solution.py:80
  3.6 9.0 %collective-permute-start.3 = (bf16[1024,128]{1,0:T(8,128)(2,1)}, bf16[1024,128]{1,0:T(8,128)(2,1)S(1)}, u32[]{:S(2)}, u32[]{:S(2)}) collective-permute-start(bf16[1024,128]{1,0:T(8,128)(2,1)} %refs_0_.3), channel_id=1, source_target_pairs={{0,4},{1,13},{2,18},{3,51},{4,8},{5,1},{6,22},{7,55},{8,12},{9,5},... | collective-permute-start | bytes 786440 | tf_op jit(solution)/shard_map/ppermute | solution.py:80
  6.3 9.9 %collective-permute-start.4 = (bf16[1024,128]{1,0:T(8,128)(2,1)}, bf16[1024,128]{1,0:T(8,128)(2,1)S(1)}, u32[]{:S(2)}, u32[]{:S(2)}) collective-permute-start(bf16[1024,128]{1,0:T(8,128)(2,1)} %refs_0_.3), channel_id=1, source_target_pairs={{0,16},{1,49},{2,6},{3,15},{4,20},{5,53},{6,10},{7,3},{8,24},{9,57... | collective-permute-start | bytes 786440 | tf_op jit(solution)/shard_map/ppermute | solution.py:80
  10.1 7.2 %collective-permute-start = (bf16[1024,128]{1,0:T(8,128)(2,1)}, bf16[1024,128]{1,0:T(8,128)(2,1)S(1)}, u32[]{:S(2)}, u32[]{:S(2)}) collective-permute-start(bf16[1024,128]{1,0:T(8,128)(2,1)} %refs_0_.3), channel_id=1, source_target_pairs={{0,48},{1,17},{2,14},{3,7},{4,52},{5,21},{6,2},{7,11},{8,56},{9,25... | collective-permute-start | bytes 786440 | tf_op jit(solution)/shard_map/ppermute | solution.py:80
  10.1 7.2 %collective-permute-start.1 = (bf16[1024,128]{1,0:T(8,128)(2,1)}, bf16[1024,128]{1,0:T(8,128)(2,1)S(1)}, u32[]{:S(2)}, u32[]{:S(2)}) collective-permute-start(bf16[1024,128]{1,0:T(8,128)(2,1)} %refs_0_.3), channel_id=1, source_target_pairs={{0,12},{1,5},{2,50},{3,19},{4,0},{5,9},{6,54},{7,23},{8,4},{9,13},... | collective-permute-start | bytes 786440 | tf_op jit(solution)/shard_map/ppermute | solution.py:80
  10.8 6.5 %collective-permute-start.5 = (s32[3,64]{1,0:T(4,128)S(1)}, s32[3,64]{1,0:T(4,128)S(1)}, u32[]{:S(2)}, u32[]{:S(2)}) collective-permute-start(s32[3,64]{1,0:T(4,128)S(1)} %pad_add_fusion.codes), channel_id=1, source_target_pairs={{0,1},{1,0},{2,3},{3,2},{4,5},{5,4},{6,7},{7,6},{8,9},{9,8},{10,11... | collective-permute-start | bytes 2312 | tf_op jit(solution)/shard_map/ppermute | solution.py:80
  17.3 12.6 %collective-permute-start.10 = (bf16[2048,128]{1,0:T(8,128)(2,1)}, bf16[2048,128]{1,0:T(8,128)(2,1)S(1)}, u32[]{:S(2)}, u32[]{:S(2)}) collective-permute-start(bf16[2048,128]{1,0:T(8,128)(2,1)} %get-tuple-element.39), channel_id=1, source_target_pairs={{0,4},{1,13},{2,18},{3,51},{4,8},{5,1},{6,22},{7,55},{8,12},{9,5},... | collective-permute-start | bytes 1572872 | tf_op jit(solution)/shard_map/ppermute | solution.py:80
  18.5 12.8 %collective-permute-start.9 = (bf16[2048,128]{1,0:T(8,128)(2,1)}, bf16[2048,128]{1,0:T(8,128)(2,1)S(1)}, u32[]{:S(2)}, u32[]{:S(2)}) collective-permute-start(bf16[2048,128]{1,0:T(8,128)(2,1)} %get-tuple-element.38), channel_id=1, source_target_pairs={{0,48},{1,17},{2,14},{3,7},{4,52},{5,21},{6,2},{7,11},{8,56},{9,25... | collective-permute-start | bytes 1572872 | tf_op jit(solution)/shard_map/ppermute | solution.py:80
  18.6 12.9 %collective-permute-start.8 = (bf16[2048,128]{1,0:T(8,128)(2,1)S(1)}, bf16[2048,128]{1,0:T(8,128)(2,1)S(1)}, u32[]{:S(2)}, u32[]{:S(2)}) collective-permute-start(bf16[2048,128]{1,0:T(8,128)(2,1)S(1)} %constant_dynamic-update-slice_fusion.2.refs_2_), channel_id=1, source_target_pairs={{0,2},{1,3},{2,0},{3,1},{4,6},{5,7},{6,4},{7,5},{8,10},{9,11},{10,... | collective-permute-start | bytes 1572872 | tf_op jit(solution)/shard_map/ppermute | solution.py:80
  20.4 13.7 %collective-permute-start.7 = (bf16[2048,128]{1,0:T(8,128)(2,1)S(1)}, bf16[2048,128]{1,0:T(8,128)(2,1)}, u32[]{:S(2)}, u32[]{:S(2)}) collective-permute-start(bf16[2048,128]{1,0:T(8,128)(2,1)S(1)} %constant_dynamic-update-slice_fusion.refs_1_), channel_id=1, source_target_pairs={{0,16},{1,49},{2,6},{3,15},{4,20},{5,53},{6,10},{7,3},{8,24},{9,57... | collective-permute-start | bytes 1572872 | tf_op jit(solution)/shard_map/ppermute | solution.py:80
  22.3 11.7 %collective-permute-start.6 = (bf16[2048,128]{1,0:T(8,128)(2,1)}, bf16[2048,128]{1,0:T(8,128)(2,1)S(1)}, u32[]{:S(2)}, u32[]{:S(2)}) collective-permute-start(bf16[2048,128]{1,0:T(8,128)(2,1)} %pad_maximum_fusion), channel_id=1, source_target_pairs={{0,12},{1,5},{2,50},{3,19},{4,0},{5,9},{6,54},{7,23},{8,4},{9,13},... | collective-permute-start | bytes 1572872 | tf_op jit(solution)/shard_map/ppermute | solution.py:80
  23.3 5.9 %copy-start.1 = (bf16[1024,128]{1,0:T(8,128)(2,1)S(1)}, bf16[1024,128]{1,0:T(8,128)(2,1)}, u32[]{:S(2)}) copy-start(bf16[1024,128]{1,0:T(8,128)(2,1)} %refs_0_.3) | copy-start | bytes 786436
  35.5 4.6 %collective-permute-start.12 = (bf16[32,256,128]{2,1,0:T(8,128)(2,1)S(1)}, bf16[32,256,128]{2,1,0:T(8,128)(2,1)S(1)}, u32[]{:S(2)}, u32[]{:S(2)}) collective-permute-start(bf16[32,256,128]{2,1,0:T(8,128)(2,1)S(1)} %pack.5), channel_id=1, source_target_pairs={{0,1},{1,0},{2,3},{3,2},{4,5},{5,4},{6,7},{7,6},{8,9},{9,8},{10,11... | collective-permute-start | bytes 6291464 | tf_op jit(solution)/shard_map/ppermute | solution.py:80
  36.4 10.9 %collective-permute-start.15 = (bf16[2048,128]{1,0:T(8,128)(2,1)S(1)}, bf16[2048,128]{1,0:T(8,128)(2,1)S(1)}, u32[]{:S(2)}, u32[]{:S(2)}) collective-permute-start(bf16[2048,128]{1,0:T(8,128)(2,1)S(1)} %pad_maximum_fusion.5), channel_id=1, source_target_pairs={{0,48},{1,17},{2,14},{3,7},{4,52},{5,21},{6,2},{7,11},{8,56},{9,25... | collective-permute-start | bytes 1572872 | tf_op jit(solution)/shard_map/ppermute | solution.py:80
  37.2 10.1 %collective-permute-start.14 = (bf16[2048,128]{1,0:T(8,128)(2,1)S(1)}, bf16[2048,128]{1,0:T(8,128)(2,1)S(1)}, u32[]{:S(2)}, u32[]{:S(2)}) collective-permute-start(bf16[2048,128]{1,0:T(8,128)(2,1)S(1)} %pad_maximum_fusion.4), channel_id=1, source_target_pairs={{0,4},{1,13},{2,18},{3,51},{4,8},{5,1},{6,22},{7,55},{8,12},{9,5},... | collective-permute-start | bytes 1572872 | tf_op jit(solution)/shard_map/ppermute | solution.py:80
  37.9 12.2 %collective-permute-start.11 = (bf16[2048,128]{1,0:T(8,128)(2,1)S(1)}, bf16[2048,128]{1,0:T(8,128)(2,1)S(1)}, u32[]{:S(2)}, u32[]{:S(2)}) collective-permute-start(bf16[2048,128]{1,0:T(8,128)(2,1)S(1)} %collective-permute-done.6.refs_1_.refs_5_), channel_id=1, source_target_pairs={{0,2},{1,3},{2,0},{3,1},{4,6},{5,7},{6,4},{7,5},{8,10},{9,11},{10,... | collective-permute-start | bytes 1572872 | tf_op jit(solution)/shard_map/ppermute | solution.py:80
  40.1 10.9 %collective-permute-start.16 = (bf16[2048,128]{1,0:T(8,128)(2,1)S(1)}, bf16[2048,128]{1,0:T(8,128)(2,1)S(1)}, u32[]{:S(2)}, u32[]{:S(2)}) collective-permute-start(bf16[2048,128]{1,0:T(8,128)(2,1)S(1)} %collective-permute-done.10.refs_4_.refs_8_), channel_id=1, source_target_pairs={{0,16},{1,49},{2,6},{3,15},{4,20},{5,53},{6,10},{7,3},{8,24},{9,57... | collective-permute-start | bytes 1572872 | tf_op jit(solution)/shard_map/ppermute | solution.py:80
  42.3 12.3 %collective-permute-start.13 = (bf16[2048,128]{1,0:T(8,128)(2,1)S(1)}, bf16[2048,128]{1,0:T(8,128)(2,1)S(1)}, u32[]{:S(2)}, u32[]{:S(2)}) collective-permute-start(bf16[2048,128]{1,0:T(8,128)(2,1)S(1)} %collective-permute-done.8.refs_2_.refs_6_), channel_id=1, source_target_pairs={{0,12},{1,5},{2,50},{3,19},{4,0},{5,9},{6,54},{7,23},{8,4},{9,13},... | collective-permute-start | bytes 1572872 | tf_op jit(solution)/shard_map/ppermute | solution.py:80
  55.4 4.7 %collective-permute-start.21 = (bf16[20,256,128]{2,1,0:T(8,128)(2,1)S(1)}, bf16[20,256,128]{2,1,0:T(8,128)(2,1)S(1)}, u32[]{:S(2)}, u32[]{:S(2)}) collective-permute-start(bf16[20,256,128]{2,1,0:T(8,128)(2,1)S(1)} %pack.6), channel_id=1, source_target_pairs={{0,1},{1,0},{2,3},{3,2},{4,5},{5,4},{6,7},{7,6},{8,9},{9,8},{10,11... | collective-permute-start | bytes 3932168 | tf_op jit(solution)/shard_map/ppermute | solution.py:80
  55.6 11.4 %collective-permute-start.17 = (bf16[2048,128]{1,0:T(8,128)(2,1)S(1)}, bf16[2048,128]{1,0:T(8,128)(2,1)S(1)}, u32[]{:S(2)}, u32[]{:S(2)}) collective-permute-start(bf16[2048,128]{1,0:T(8,128)(2,1)S(1)} %pad_maximum_fusion.3), channel_id=1, source_target_pairs={{0,12},{1,5},{2,50},{3,19},{4,0},{5,9},{6,54},{7,23},{8,4},{9,13},... | collective-permute-start | bytes 1572872 | tf_op jit(solution)/shard_map/ppermute | solution.py:80
  56.0 8.6 %collective-permute-start.20 = (bf16[1024,128]{1,0:T(8,128)(2,1)S(1)}, bf16[1024,128]{1,0:T(8,128)(2,1)S(1)}, u32[]{:S(2)}, u32[]{:S(2)}) collective-permute-start(bf16[1024,128]{1,0:T(8,128)(2,1)S(1)} %slice.45), channel_id=1, source_target_pairs={{0,48},{1,17},{2,14},{3,7},{4,52},{5,21},{6,2},{7,11},{8,56},{9,25... | collective-permute-start | bytes 786440 | tf_op jit(solution)/shard_map/ppermute | solution.py:80
  57.5 8.0 %collective-permute-start.19 = (bf16[1024,128]{1,0:T(8,128)(2,1)S(1)}, bf16[1024,128]{1,0:T(8,128)(2,1)S(1)}, u32[]{:S(2)}, u32[]{:S(2)}) collective-permute-start(bf16[1024,128]{1,0:T(8,128)(2,1)S(1)} %slice.44), channel_id=1, source_target_pairs={{0,2},{1,3},{2,0},{3,1},{4,6},{5,7},{6,4},{7,5},{8,10},{9,11},{10,... | collective-permute-start | bytes 786440 | tf_op jit(solution)/shard_map/ppermute | solution.py:80
  59.3 7.7 %collective-permute-start.18 = (bf16[1024,128]{1,0:T(8,128)(2,1)S(1)}, bf16[1024,128]{1,0:T(8,128)(2,1)S(1)}, u32[]{:S(2)}, u32[]{:S(2)}) collective-permute-start(bf16[1024,128]{1,0:T(8,128)(2,1)S(1)} %get-tuple-element.56), channel_id=1, source_target_pairs={{0,32},{1,33},{2,10},{3,11},{4,36},{5,37},{6,14},{7,15},{8,40},{9,... | collective-permute-start | bytes 786440 | tf_op jit(solution)/shard_map/ppermute | solution.py:80
  60.1 7.9 %collective-permute-start.22 = (bf16[1024,128]{1,0:T(8,128)(2,1)S(1)}, bf16[1024,128]{1,0:T(8,128)(2,1)S(1)}, u32[]{:S(2)}, u32[]{:S(2)}) collective-permute-start(bf16[1024,128]{1,0:T(8,128)(2,1)S(1)} %slice.37), channel_id=1, source_target_pairs={{0,4},{1,13},{2,18},{3,51},{4,8},{5,1},{6,22},{7,55},{8,12},{9,5},... | collective-permute-start | bytes 786440 | tf_op jit(solution)/shard_map/ppermute | solution.py:80
  68.7 3.5 %collective-permute-start.23 = (bf16[12,256,128]{2,1,0:T(8,128)(2,1)S(1)}, bf16[12,256,128]{2,1,0:T(8,128)(2,1)S(1)}, u32[]{:S(2)}, u32[]{:S(2)}) collective-permute-start(bf16[12,256,128]{2,1,0:T(8,128)(2,1)S(1)} %pack.7), channel_id=1, source_target_pairs={{0,1},{1,0},{2,3},{3,2},{4,5},{5,4},{6,7},{7,6},{8,9},{9,8},{10,11... | collective-permute-start | bytes 2359304 | tf_op jit(solution)/shard_map/ppermute | solution.py:80
  73.4 7.5 %copy-start.2 = (f32[256]{0:T(256)S(1)}, f32[256]{0:T(256)}, u32[]{:S(2)}) copy-start(f32[256]{0:T(256)} %param.11) | copy-start | bytes 3076
  73.4 7.5 %collective-permute-start.24 = (bf16[1024,128]{1,0:T(8,128)(2,1)S(1)}, bf16[1024,128]{1,0:T(8,128)(2,1)S(1)}, u32[]{:S(2)}, u32[]{:S(2)}) collective-permute-start(bf16[1024,128]{1,0:T(8,128)(2,1)S(1)} %convert_element_type.12), channel_id=1, source_target_pairs={{0,64},{64,0},{1,65},{65,1},{2,66},{66,2},{3,67},{67,3},{4,68},{68... | collective-permute-start | bytes 786440 | tf_op jit(solution)/shard_map/ppermute | solution.py:351
